TPU v7x, 32 devices: a whole 2x2x4 slice. The times are simulated.
32 devices in a mesh: slab: 8 (over z, y), case: 4 (over x, core).
Axes of the slice: x: 2, y: 2, z: 4, core: 2. Of those that a mesh axis runs over, the one named last changes fastest.
Arguments:
- pressure: float32 [64, 512], replicated, may hold values from -9 to 9
- panel: int32 [96, 4, 128], P('slab'), may hold values from 0 to 511
- flags: int32 [96, 4, 128], P('slab'), may hold values 0 or 1
- diagonal: float32 [96, 4, 128], P('slab'), may hold values from 0.25 to 4
Outputs:
- fields: float32 [64, 96, 4, 128], P('case', 'slab')
- gram: float32 [64, 64], P('case')
- cross: float32 [64, 64], P('case')
All inputs are finite; a program needn't handle non-finite values. No bound on the sum of `flags` on one device may be relied on, other than what follows from the above.
Results may differ from a plain program's by a relative error of at most 0.00005.
Values sent between devices are 32-bit elements; how exact they have to be, the bound alone decides.
No kernel may reach another device: no remote copies, remote signals or barrier semaphores. Data moves between devices by JAX's collectives and lax.ppermute only.
A program may use at most 64 MiB of HBM per device.

v0:
```python
import jax
import jax.numpy as jnp
from jax import lax
from jax.sharding import PartitionSpec as P

damping = 0.7
penalty = 4.0
highest = lax.Precision.HIGHEST


def with_halo(cells, sides, width):
    for axis, dim in sides:
        count = lax.axis_size(axis)
        ends = count - 1
        head = lax.slice_in_dim(cells, 0, width, axis=dim)
        tail = lax.slice_in_dim(cells, cells.shape[dim] - width, cells.shape[dim], axis=dim)
        cells = jnp.concatenate(
            [
                lax.ppermute(tail, axis, [(i, (i + 1) % count) for i in range(ends)]),
                cells,
                lax.ppermute(head, axis, [((i + 1) % count, i) for i in range(ends)]),
            ],
            axis=dim,
        )
    return cells


def from_behind(x, axis, by):
    count = lax.axis_size(axis)
    pairs = [(i, i + by) for i in range(count) if 0 <= i + by < count]
    return lax.ppermute(x, axis, pairs)


def transverse(field):
    beside_all = jnp.roll(field, 1, axis=-1) + jnp.roll(field, -1, axis=-1)
    zero_row = jnp.zeros_like(field[..., :1, :])
    inward = jnp.concatenate([zero_row, field[..., :-1, :]], axis=-2)
    outward = jnp.concatenate([field[..., 1:, :], zero_row], axis=-2)
    return beside_all + inward + outward


def stencil(field, below, above, coeff, weight):
    return (coeff + 2.0 * weight + 4.0) * field - weight * (below + above) - transverse(field)


def apply_halo(field, coeff, weight):
    padded = with_halo(field, (("slab", 1),), 1)
    return stencil(field, padded[:, :-2], padded[:, 2:], coeff, weight)


def smooth_halo(field, rhs, coeff, weight):
    return field + damping * (rhs - apply_halo(field, coeff, weight)) / (coeff + 2.0 * weight + 4.0)


def restrict(fine):
    even = fine[:, 0::2]
    odd = fine[:, 1::2]
    lower = from_behind(fine[:, -1:], "slab", 1)
    odd_before = jnp.concatenate([lower, odd[:, :-1]], axis=1)
    return 0.5 * even + 0.25 * (odd + odd_before)


def prolong(coarse):
    upper = from_behind(coarse[:, :1], "slab", -1)
    following = jnp.concatenate([coarse[:, 1:], upper], axis=1)
    middle = 0.5 * (coarse + following)
    stacked = jnp.stack([coarse, middle], axis=2)
    shape = coarse.shape
    return stacked.reshape(shape[0], 2 * shape[1], shape[2], shape[3])


def coarsest(rhs, coeff, weight):
    field = damping * rhs / (coeff + 2.0 * weight + 4.0)
    for sweep in range(3):
        field = smooth_halo(field, rhs, coeff, weight)
    return field


def vcycle(rhs, coeff, level):
    weight = 0.25**level
    if level == 2:
        return coarsest(rhs, coeff, weight)
    field = damping * rhs / (coeff + 2.0 * weight + 4.0)
    field = smooth_halo(field, rhs, coeff, weight)
    leftover = rhs - apply_halo(field, coeff, weight)
    coarse_coeff = 0.5 * (coeff[0::2] + coeff[1::2])
    field = field + prolong(vcycle(restrict(leftover), coarse_coeff, level + 1))
    for sweep in range(2):
        field = smooth_halo(field, rhs, coeff, weight)
    return field


def local(pressure, panel, flags, diagonal):
    layers, radial, beside_all = panel.shape
    slabs = lax.axis_size("slab")
    groups = lax.axis_size("case")
    per_group = pressure.shape[0] // groups
    total_layers = layers * slabs
    own_group = lax.axis_index("case")
    case_rows = lax.dynamic_slice_in_dim(pressure, own_group * per_group, per_group, 0)
    coeff = diagonal + penalty * flags.astype(jnp.float32)
    keep = 1.0 - flags.astype(jnp.float32)
    positions = (lax.axis_index("slab") * layers + jnp.arange(layers)).astype(jnp.float32)
    span = (1.0 + 2.0 * positions / total_layers)[:, None, None]
    loads = jnp.take(case_rows, panel, axis=1) * span * keep
    fields = vcycle(loads, coeff, 0)
    images = apply_halo(fields, coeff, 1.0)
    scale = 1.0 / (total_layers * radial * beside_all)
    contract = (((1,), (1,)), ((), ()))
    images_flat = images.reshape(per_group, -1)
    loads_flat = loads.reshape(per_group, -1)
    piece = lax.all_gather(fields, "case", axis=0, tiled=True)
    piece_flat = piece.reshape(piece.shape[0], -1)
    gram_block = lax.dot_general(
        images_flat, piece_flat, contract, precision=highest, preferred_element_type=jnp.float32
    )
    cross_block = lax.dot_general(
        loads_flat, piece_flat, contract, precision=highest, preferred_element_type=jnp.float32
    )
    gram_rows, cross_rows = lax.psum((gram_block, cross_block), "slab")
    return (fields, gram_rows * scale, cross_rows * scale)


def solution(mesh):
    in_specs = (P(), P("slab", None, None), P("slab", None, None), P("slab", None, None))
    out_specs = (P("case", "slab", None, None), P("case", None), P("case", None))
    return jax.shard_map(local, mesh=mesh, in_specs=in_specs, out_specs=out_specs, check_vma=False)
```

profile of v0, /device:TPU:0, one launch (start us, length us, event | category | flops | bytes accessed | tf_op | source)
XLA Modules:
  0.0 236.3 jit_solution(16116104396170386589)
XLA Ops:
  7.2 0.8 compare_select_fusion
  8.0 0.8 compare_and_fusion
  8.9 20.9 %gather_fusion = f32[6144,16]{1,0:T(8,128)} fusion(f32[16,512]{0,1:T(8,128)S(1)} %copy.21, s32[6144]{0:T(1024)S(1)} %broadcast_clamp_fusion), kind=kCustom, calls=%fused_computation | custom fusion | bytes 811008 | tf_op jit(solution)/shard_map/jit(_take)/gather | solution.py:105
  29.9 2.3 copy.13
  32.4 4.9 %collective-permute-start = (f32[16,1,4,128]{3,0,2,1:T(8,128)S(1)}, f32[16,1,4,128]{3,0,2,1:T(8,128)S(1)}, u32[]{:S(2)}, u32[]{:S(2)}) collective-permute-start(f32[16,1,4,128]{3,0,2,1:T(8,128)S(1)} %get-tuple-element.57), channel_id=1, source_target_pairs={{0,4},{4,8},{8,12},{12,16},{16,20},{20,24},{24,28},{1,5},{5,9},{9,... | collective-permute-start | bytes 98312 | tf_op jit(solution)/shard_map/ppermute | solution.py:19
  37.3 1.3 collective-permute-start.1
  39.0 4.1 %collective-permute-done.1 = f32[16,1,4,128]{3,0,2,1:T(8,128)S(1)} collective-permute-done((f32[16,1,4,128]{3,0,2,1:T(8,128)S(1)}, f32[16,1,4,128]{3,0,2,1:T(8,128)S(1)}, u32[]{:S(2)}, u32[]{:S(2)}) %collective-permute-start.1) | collective-permute-done | bytes 32800 | tf_op jit(solution)/shard_map/ppermute | solution.py:21
  43.1 0.5 fusion.30
  44.0 4.3 %collective-permute-start.2 = (f32[16,1,4,128]{3,0,2,1:T(8,128)S(1)}, f32[16,1,4,128]{3,0,2,1:T(8,128)S(1)}, u32[]{:S(2)}, u32[]{:S(2)}) collective-permute-start(f32[16,1,4,128]{3,0,2,1:T(8,128)S(1)} %get-tuple-element.49), channel_id=1, source_target_pairs={{0,4},{4,8},{8,12},{12,16},{16,20},{20,24},{24,28},{1,5},{5,9},{9,... | collective-permute-start | bytes 98312 | tf_op jit(solution)/shard_map/ppermute | solution.py:19
  48.3 1.3 collective-permute-start.3
  49.9 4.2 %collective-permute-done.3 = f32[16,1,4,128]{3,0,2,1:T(8,128)S(1)} collective-permute-done((f32[16,1,4,128]{3,0,2,1:T(8,128)S(1)}, f32[16,1,4,128]{3,0,2,1:T(8,128)S(1)}, u32[]{:S(2)}, u32[]{:S(2)}) %collective-permute-start.3) | collective-permute-done | bytes 32800 | tf_op jit(solution)/shard_map/ppermute | solution.py:21
  54.1 0.4 fusion.23
  54.5 3.4 %collective-permute-start.4 = (f32[16,1,4,128]{3,0,2,1:T(8,128)S(1)}, f32[16,1,4,128]{3,0,2,1:T(8,128)S(1)}, u32[]{:S(2)}, u32[]{:S(2)}) collective-permute-start(f32[16,1,4,128]{3,0,2,1:T(8,128)S(1)} %slice.598), channel_id=1, source_target_pairs={{0,4},{4,8},{8,12},{12,16},{16,20},{20,24},{24,28},{1,5},{5,9},{9,... | collective-permute-start | bytes 98312 | tf_op jit(solution)/shard_map/ppermute | solution.py:31
  58.0 1.5 collective-permute-done.4
  59.9 4.2 %collective-permute-start.5 = (f32[16,1,4,128]{3,0,2,1:T(8,128)S(1)}, f32[16,1,4,128]{3,0,2,1:T(8,128)S(1)}, u32[]{:S(2)}, u32[]{:S(2)}) collective-permute-start(f32[16,1,4,128]{3,0,2,1:T(8,128)S(1)} %get-tuple-element.89), channel_id=1, source_target_pairs={{0,4},{4,8},{8,12},{12,16},{16,20},{20,24},{24,28},{1,5},{5,9},{9,... | collective-permute-start | bytes 98312 | tf_op jit(solution)/shard_map/ppermute | solution.py:19
  64.1 1.3 collective-permute-start.6
  65.4 0.3 collective-permute-done.5
  65.7 4.6 %collective-permute-done.6 = f32[16,1,4,128]{3,0,2,1:T(8,128)S(1)} collective-permute-done((f32[16,1,4,128]{3,0,2,1:T(8,128)S(1)}, f32[16,1,4,128]{3,0,2,1:T(8,128)S(1)}, u32[]{:S(2)}, u32[]{:S(2)}) %collective-permute-start.6) | collective-permute-done | bytes 32800 | tf_op jit(solution)/shard_map/ppermute | solution.py:21
  70.7 4.9 %collective-permute-start.7 = (f32[16,1,4,128]{3,0,2,1:T(8,128)S(1)}, f32[16,1,4,128]{3,0,2,1:T(8,128)S(1)}, u32[]{:S(2)}, u32[]{:S(2)}) collective-permute-start(f32[16,1,4,128]{3,0,2,1:T(8,128)S(1)} %get-tuple-element.81), channel_id=1, source_target_pairs={{0,4},{4,8},{8,12},{12,16},{16,20},{20,24},{24,28},{1,5},{5,9},{9,... | collective-permute-start | bytes 98312 | tf_op jit(solution)/shard_map/ppermute | solution.py:19
  75.6 1.3 collective-permute-start.8
  77.2 4.2 %collective-permute-done.8 = f32[16,1,4,128]{3,0,2,1:T(8,128)S(1)} collective-permute-done((f32[16,1,4,128]{3,0,2,1:T(8,128)S(1)}, f32[16,1,4,128]{3,0,2,1:T(8,128)S(1)}, u32[]{:S(2)}, u32[]{:S(2)}) %collective-permute-start.8) | collective-permute-done | bytes 32800 | tf_op jit(solution)/shard_map/ppermute | solution.py:21
  81.6 2.9 %collective-permute-start.9 = (f32[16,1,4,128]{3,0,2,1:T(8,128)S(1)}, f32[16,1,4,128]{3,0,2,1:T(8,128)S(1)}, u32[]{:S(2)}, u32[]{:S(2)}) collective-permute-start(f32[16,1,4,128]{3,0,2,1:T(8,128)S(1)} %slice.616), channel_id=1, source_target_pairs={{0,4},{4,8},{8,12},{12,16},{16,20},{20,24},{24,28},{1,5},{5,9},{9,... | collective-permute-start | bytes 98312 | tf_op jit(solution)/shard_map/ppermute | solution.py:31
  84.6 1.5 collective-permute-done.9
  86.4 4.2 %collective-permute-start.10 = (f32[16,1,4,128]{3,0,2,1:T(8,128)S(1)}, f32[16,1,4,128]{3,0,2,1:T(8,128)S(1)}, u32[]{:S(2)}, u32[]{:S(2)}) collective-permute-start(f32[16,1,4,128]{3,0,2,1:T(8,128)S(1)} %get-tuple-element.113), channel_id=1, source_target_pairs={{0,4},{4,8},{8,12},{12,16},{16,20},{20,24},{24,28},{1,5},{5,9},{9,... | collective-permute-start | bytes 98312 | tf_op jit(solution)/shard_map/ppermute | solution.py:19
  90.6 1.3 collective-permute-start.11
  91.9 0.3 collective-permute-done.10
  92.2 5.4 %collective-permute-done.11 = f32[16,1,4,128]{3,0,2,1:T(8,128)S(1)} collective-permute-done((f32[16,1,4,128]{3,0,2,1:T(8,128)S(1)}, f32[16,1,4,128]{3,0,2,1:T(8,128)S(1)}, u32[]{:S(2)}, u32[]{:S(2)}) %collective-permute-start.11) | collective-permute-done | bytes 32800 | tf_op jit(solution)/shard_map/ppermute | solution.py:21
  97.9 4.6 %collective-permute-start.12 = (f32[16,1,4,128]{3,0,2,1:T(8,128)S(1)}, f32[16,1,4,128]{3,0,2,1:T(8,128)S(1)}, u32[]{:S(2)}, u32[]{:S(2)}) collective-permute-start(f32[16,1,4,128]{3,0,2,1:T(8,128)S(1)} %get-tuple-element.105), channel_id=1, source_target_pairs={{0,4},{4,8},{8,12},{12,16},{16,20},{20,24},{24,28},{1,5},{5,9},{9,... | collective-permute-start | bytes 98312 | tf_op jit(solution)/shard_map/ppermute | solution.py:19
  102.5 1.3 collective-permute-start.13
  103.8 0.3 collective-permute-done.12
  104.1 4.2 %collective-permute-done.13 = f32[16,1,4,128]{3,0,2,1:T(8,128)S(1)} collective-permute-done((f32[16,1,4,128]{3,0,2,1:T(8,128)S(1)}, f32[16,1,4,128]{3,0,2,1:T(8,128)S(1)}, u32[]{:S(2)}, u32[]{:S(2)}) %collective-permute-start.13) | collective-permute-done | bytes 32800 | tf_op jit(solution)/shard_map/ppermute | solution.py:21
  108.6 2.8 %collective-permute-start.14 = (f32[16,1,4,128]{3,0,2,1:T(8,128)S(1)}, f32[16,1,4,128]{3,0,2,1:T(8,128)S(1)}, u32[]{:S(2)}, u32[]{:S(2)}) collective-permute-start(f32[16,1,4,128]{3,0,2,1:T(8,128)S(1)} %get-tuple-element.97), channel_id=1, source_target_pairs={{0,4},{4,8},{8,12},{12,16},{16,20},{20,24},{24,28},{1,5},{5,9},{9,... | collective-permute-start | bytes 98312 | tf_op jit(solution)/shard_map/ppermute | solution.py:19
  111.5 1.3 collective-permute-start.15
  112.8 0.3 collective-permute-done.14
  113.0 4.2 %collective-permute-done.15 = f32[16,1,4,128]{3,0,2,1:T(8,128)S(1)} collective-permute-done((f32[16,1,4,128]{3,0,2,1:T(8,128)S(1)}, f32[16,1,4,128]{3,0,2,1:T(8,128)S(1)}, u32[]{:S(2)}, u32[]{:S(2)}) %collective-permute-start.15) | collective-permute-done | bytes 32800 | tf_op jit(solution)/shard_map/ppermute | solution.py:21
  117.4 1.3 collective-permute-start.16
  118.7 4.5 %collective-permute-done.16 = f32[16,1,4,128]{3,0,2,1:T(8,128)S(1)} collective-permute-done((f32[16,1,4,128]{3,0,2,1:T(8,128)S(1)}, f32[16,1,4,128]{3,0,2,1:T(8,128)S(1)}, u32[]{:S(2)}, u32[]{:S(2)}) %collective-permute-start.16) | collective-permute-done | bytes 32800 | tf_op jit(solution)/shard_map/ppermute | solution.py:31
  123.6 4.4 %collective-permute-start.17 = (f32[16,1,4,128]{3,0,2,1:T(8,128)S(1)}, f32[16,1,4,128]{3,0,2,1:T(8,128)S(1)}, u32[]{:S(2)}, u32[]{:S(2)}) collective-permute-start(f32[16,1,4,128]{3,0,2,1:T(8,128)S(1)} %get-tuple-element.73), channel_id=1, source_target_pairs={{0,4},{4,8},{8,12},{12,16},{16,20},{20,24},{24,28},{1,5},{5,9},{9,... | collective-permute-start | bytes 98312 | tf_op jit(solution)/shard_map/ppermute | solution.py:19
  128.0 1.3 collective-permute-start.18
  129.3 0.2 collective-permute-done.17
  129.6 4.2 %collective-permute-done.18 = f32[16,1,4,128]{3,0,2,1:T(8,128)S(1)} collective-permute-done((f32[16,1,4,128]{3,0,2,1:T(8,128)S(1)}, f32[16,1,4,128]{3,0,2,1:T(8,128)S(1)}, u32[]{:S(2)}, u32[]{:S(2)}) %collective-permute-start.18) | collective-permute-done | bytes 32800 | tf_op jit(solution)/shard_map/ppermute | solution.py:21
  134.2 2.9 %collective-permute-start.19 = (f32[16,1,4,128]{3,0,2,1:T(8,128)S(1)}, f32[16,1,4,128]{3,0,2,1:T(8,128)S(1)}, u32[]{:S(2)}, u32[]{:S(2)}) collective-permute-start(f32[16,1,4,128]{3,0,2,1:T(8,128)S(1)} %get-tuple-element.65), channel_id=1, source_target_pairs={{0,4},{4,8},{8,12},{12,16},{16,20},{20,24},{24,28},{1,5},{5,9},{9,... | collective-permute-start | bytes 98312 | tf_op jit(solution)/shard_map/ppermute | solution.py:19
  137.2 1.3 collective-permute-start.20
  138.5 0.2 collective-permute-done.19
  138.7 4.2 %collective-permute-done.20 = f32[16,1,4,128]{3,0,2,1:T(8,128)S(1)} collective-permute-done((f32[16,1,4,128]{3,0,2,1:T(8,128)S(1)}, f32[16,1,4,128]{3,0,2,1:T(8,128)S(1)}, u32[]{:S(2)}, u32[]{:S(2)}) %collective-permute-start.20) | collective-permute-done | bytes 32800 | tf_op jit(solution)/shard_map/ppermute | solution.py:21
  143.2 1.3 collective-permute-start.21
  144.5 4.5 %collective-permute-done.21 = f32[16,1,4,128]{3,0,2,1:T(8,128)S(1)} collective-permute-done((f32[16,1,4,128]{3,0,2,1:T(8,128)S(1)}, f32[16,1,4,128]{3,0,2,1:T(8,128)S(1)}, u32[]{:S(2)}, u32[]{:S(2)}) %collective-permute-start.21) | collective-permute-done | bytes 32800 | tf_op jit(solution)/shard_map/ppermute | solution.py:31
  149.5 3.7 %collective-permute-start.22 = (f32[16,1,4,128]{3,0,2,1:T(8,128)S(1)}, f32[16,1,4,128]{3,0,2,1:T(8,128)S(1)}, u32[]{:S(2)}, u32[]{:S(2)}) collective-permute-start(f32[16,1,4,128]{3,0,2,1:T(8,128)S(1)} %get-tuple-element.41), channel_id=1, source_target_pairs={{0,4},{4,8},{8,12},{12,16},{16,20},{20,24},{24,28},{1,5},{5,9},{9,... | collective-permute-start | bytes 98312 | tf_op jit(solution)/shard_map/ppermute | solution.py:19
  153.3 1.3 collective-permute-start.23
  154.8 4.2 %collective-permute-done.23 = f32[16,1,4,128]{3,0,2,1:T(8,128)S(1)} collective-permute-done((f32[16,1,4,128]{3,0,2,1:T(8,128)S(1)}, f32[16,1,4,128]{3,0,2,1:T(8,128)S(1)}, u32[]{:S(2)}, u32[]{:S(2)}) %collective-permute-start.23) | collective-permute-done | bytes 32800 | tf_op jit(solution)/shard_map/ppermute | solution.py:21
  159.1 0.5 fusion.19
  159.9 2.9 %collective-permute-start.24 = (f32[16,1,4,128]{3,0,2,1:T(8,128)S(1)}, f32[16,1,4,128]{3,0,2,1:T(8,128)S(1)}, u32[]{:S(2)}, u32[]{:S(2)}) collective-permute-start(f32[16,1,4,128]{3,0,2,1:T(8,128)S(1)} %get-tuple-element.33), channel_id=1, source_target_pairs={{0,4},{4,8},{8,12},{12,16},{16,20},{20,24},{24,28},{1,5},{5,9},{9,... | collective-permute-start | bytes 98312 | tf_op jit(solution)/shard_map/ppermute | solution.py:19
  162.9 1.3 collective-permute-start.25
  164.4 4.2 %collective-permute-done.25 = f32[16,1,4,128]{3,0,2,1:T(8,128)S(1)} collective-permute-done((f32[16,1,4,128]{3,0,2,1:T(8,128)S(1)}, f32[16,1,4,128]{3,0,2,1:T(8,128)S(1)}, u32[]{:S(2)}, u32[]{:S(2)}) %collective-permute-start.25) | collective-permute-done | bytes 32800 | tf_op jit(solution)/shard_map/ppermute | solution.py:21
  168.7 1.2 fusion.12
  169.9 1.9 copy.16
  171.9 0.8 fusion.135
  172.6 2.8 %collective-permute-start.26 = (f32[16,1,4,128]{3,0,2,1:T(8,128)S(1)}, f32[16,1,4,128]{3,0,2,1:T(8,128)S(1)}, u32[]{:S(2)}, u32[]{:S(2)}) collective-permute-start(f32[16,1,4,128]{3,0,2,1:T(8,128)S(1)} %get-tuple-element.25), channel_id=1, source_target_pairs={{0,4},{4,8},{8,12},{12,16},{16,20},{20,24},{24,28},{1,5},{5,9},{9,... | collective-permute-start | bytes 98312 | tf_op jit(solution)/shard_map/ppermute | solution.py:19
  175.5 1.3 collective-permute-start.27
  177.2 10.2 %all-gather.2.cloned.1.call-done = f32[64,12,4,128]{3,0,2,1:T(8,128)} async-done(((f32[16,12,4,128]{3,0,2,1:T(8,128)}), f32[64,12,4,128]{3,0,2,1:T(8,128)}) %all-gather.2.cloned.1.call-update) | async-done | bytes 1572880 | tf_op jit(solution)/shard_map/all_gather | solution.py:112
  187.3 2.9 %convolution_bitcast_fusion = f32[16,64]{1,0:T(8,128)S(1)} fusion(f32[64,12,4,128]{3,0,2,1:T(8,128)} %all-gather.2.cloned.1.call-done, f32[12,4,128,16]{2,3,1,0:T(8,128)S(1)} %copy.13, f32[12,4,128]{2,1,0:T(4,128)S(1)} %get-tuple-element.115, f32[12]{0:T(128)S(1)} %multiply_add_fusion.2, pred[12,4,128]{2,1,0:T(4,128)(4,1)S(1)} %compare_and_fusion), kind=kOutput, calls=%fused_computation.1 | convolution fusion | flops 75792384 | bytes 2000944 | tf_op jit(solution)/shard_map/dot_general | solution.py:117
  190.3 1.4 convolution_bitcast_fusion.1
  191.7 37.1 %all-reduce.24 = (f32[16,64]{1,0:T(8,128)S(1)}, f32[16,64]{1,0:T(8,128)S(1)}) all-reduce(f32[16,64]{1,0:T(8,128)S(1)} %convolution_bitcast_fusion.1, f32[16,64]{1,0:T(8,128)S(1)} %convolution_bitcast_fusion), channel_id=1, replica_groups=mesh['slab'=8,'case'=4] {'slab'}, use_global_device_ids=true, to_apply=%region_0.1 | all-reduce | flops 2048 | bytes 16384 | tf_op jit(solution)/shard_map/psum | solution.py:120
  228.9 0.6 broadcast_multiply_fusion
  (101 shorter events, 6.5 us)
Async XLA Ops:
  7.2 1.6 copy-start
  7.2 180.2 %all-gather.2.cloned.1.call-start = ((), (), s32[]{:S(2)}) async-start(), calls=%async_computation | async-start | bytes 1966080 | tf_op jit(solution)/shard_map/all_gather | solution.py:112
  29.9 2.3 copy-start.3
  29.9 2.4 copy-start.4
  32.4 6.6 %collective-permute-start = (f32[16,1,4,128]{3,0,2,1:T(8,128)S(1)}, f32[16,1,4,128]{3,0,2,1:T(8,128)S(1)}, u32[]{:S(2)}, u32[]{:S(2)}) collective-permute-start(f32[16,1,4,128]{3,0,2,1:T(8,128)S(1)} %get-tuple-element.57), channel_id=1, source_target_pairs={{0,4},{4,8},{8,12},{12,16},{16,20},{20,24},{24,28},{1,5},{5,9},{9,... | collective-permute-start | bytes 98312 | tf_op jit(solution)/shard_map/ppermute | solution.py:19
  37.3 5.8 %collective-permute-start.1 = (f32[16,1,4,128]{3,0,2,1:T(8,128)S(1)}, f32[16,1,4,128]{3,0,2,1:T(8,128)S(1)}, u32[]{:S(2)}, u32[]{:S(2)}) collective-permute-start(f32[16,1,4,128]{3,0,2,1:T(8,128)S(1)} %get-tuple-element.58), channel_id=1, source_target_pairs={{4,0},{8,4},{12,8},{16,12},{20,16},{24,20},{28,24},{5,1},{9,5},{13... | collective-permute-start | bytes 98312 | tf_op jit(solution)/shard_map/ppermute | solution.py:21
  44.0 5.9 %collective-permute-start.2 = (f32[16,1,4,128]{3,0,2,1:T(8,128)S(1)}, f32[16,1,4,128]{3,0,2,1:T(8,128)S(1)}, u32[]{:S(2)}, u32[]{:S(2)}) collective-permute-start(f32[16,1,4,128]{3,0,2,1:T(8,128)S(1)} %get-tuple-element.49), channel_id=1, source_target_pairs={{0,4},{4,8},{8,12},{12,16},{16,20},{20,24},{24,28},{1,5},{5,9},{9,... | collective-permute-start | bytes 98312 | tf_op jit(solution)/shard_map/ppermute | solution.py:19
  48.3 5.8 %collective-permute-start.3 = (f32[16,1,4,128]{3,0,2,1:T(8,128)S(1)}, f32[16,1,4,128]{3,0,2,1:T(8,128)S(1)}, u32[]{:S(2)}, u32[]{:S(2)}) collective-permute-start(f32[16,1,4,128]{3,0,2,1:T(8,128)S(1)} %get-tuple-element.50), channel_id=1, source_target_pairs={{4,0},{8,4},{12,8},{16,12},{20,16},{24,20},{28,24},{5,1},{9,5},{13... | collective-permute-start | bytes 98312 | tf_op jit(solution)/shard_map/ppermute | solution.py:21
  54.5 5.0 %collective-permute-start.4 = (f32[16,1,4,128]{3,0,2,1:T(8,128)S(1)}, f32[16,1,4,128]{3,0,2,1:T(8,128)S(1)}, u32[]{:S(2)}, u32[]{:S(2)}) collective-permute-start(f32[16,1,4,128]{3,0,2,1:T(8,128)S(1)} %slice.598), channel_id=1, source_target_pairs={{0,4},{4,8},{8,12},{12,16},{16,20},{20,24},{24,28},{1,5},{5,9},{9,... | collective-permute-start | bytes 98312 | tf_op jit(solution)/shard_map/ppermute | solution.py:31
  59.9 5.8 %collective-permute-start.5 = (f32[16,1,4,128]{3,0,2,1:T(8,128)S(1)}, f32[16,1,4,128]{3,0,2,1:T(8,128)S(1)}, u32[]{:S(2)}, u32[]{:S(2)}) collective-permute-start(f32[16,1,4,128]{3,0,2,1:T(8,128)S(1)} %get-tuple-element.89), channel_id=1, source_target_pairs={{0,4},{4,8},{8,12},{12,16},{16,20},{20,24},{24,28},{1,5},{5,9},{9,... | collective-permute-start | bytes 98312 | tf_op jit(solution)/shard_map/ppermute | solution.py:19
  64.1 6.2 %collective-permute-start.6 = (f32[16,1,4,128]{3,0,2,1:T(8,128)S(1)}, f32[16,1,4,128]{3,0,2,1:T(8,128)S(1)}, u32[]{:S(2)}, u32[]{:S(2)}) collective-permute-start(f32[16,1,4,128]{3,0,2,1:T(8,128)S(1)} %get-tuple-element.90), channel_id=1, source_target_pairs={{4,0},{8,4},{12,8},{16,12},{20,16},{24,20},{28,24},{5,1},{9,5},{13... | collective-permute-start | bytes 98312 | tf_op jit(solution)/shard_map/ppermute | solution.py:21
  70.7 6.4 %collective-permute-start.7 = (f32[16,1,4,128]{3,0,2,1:T(8,128)S(1)}, f32[16,1,4,128]{3,0,2,1:T(8,128)S(1)}, u32[]{:S(2)}, u32[]{:S(2)}) collective-permute-start(f32[16,1,4,128]{3,0,2,1:T(8,128)S(1)} %get-tuple-element.81), channel_id=1, source_target_pairs={{0,4},{4,8},{8,12},{12,16},{16,20},{20,24},{24,28},{1,5},{5,9},{9,... | collective-permute-start | bytes 98312 | tf_op jit(solution)/shard_map/ppermute | solution.py:19
  75.6 5.8 %collective-permute-start.8 = (f32[16,1,4,128]{3,0,2,1:T(8,128)S(1)}, f32[16,1,4,128]{3,0,2,1:T(8,128)S(1)}, u32[]{:S(2)}, u32[]{:S(2)}) collective-permute-start(f32[16,1,4,128]{3,0,2,1:T(8,128)S(1)} %get-tuple-element.82), channel_id=1, source_target_pairs={{4,0},{8,4},{12,8},{16,12},{20,16},{24,20},{28,24},{5,1},{9,5},{13... | collective-permute-start | bytes 98312 | tf_op jit(solution)/shard_map/ppermute | solution.py:21
  81.6 4.5 %collective-permute-start.9 = (f32[16,1,4,128]{3,0,2,1:T(8,128)S(1)}, f32[16,1,4,128]{3,0,2,1:T(8,128)S(1)}, u32[]{:S(2)}, u32[]{:S(2)}) collective-permute-start(f32[16,1,4,128]{3,0,2,1:T(8,128)S(1)} %slice.616), channel_id=1, source_target_pairs={{0,4},{4,8},{8,12},{12,16},{16,20},{20,24},{24,28},{1,5},{5,9},{9,... | collective-permute-start | bytes 98312 | tf_op jit(solution)/shard_map/ppermute | solution.py:31
  86.4 5.8 %collective-permute-start.10 = (f32[16,1,4,128]{3,0,2,1:T(8,128)S(1)}, f32[16,1,4,128]{3,0,2,1:T(8,128)S(1)}, u32[]{:S(2)}, u32[]{:S(2)}) collective-permute-start(f32[16,1,4,128]{3,0,2,1:T(8,128)S(1)} %get-tuple-element.113), channel_id=1, source_target_pairs={{0,4},{4,8},{8,12},{12,16},{16,20},{20,24},{24,28},{1,5},{5,9},{9,... | collective-permute-start | bytes 98312 | tf_op jit(solution)/shard_map/ppermute | solution.py:19
  90.6 7.0 %collective-permute-start.11 = (f32[16,1,4,128]{3,0,2,1:T(8,128)S(1)}, f32[16,1,4,128]{3,0,2,1:T(8,128)S(1)}, u32[]{:S(2)}, u32[]{:S(2)}) collective-permute-start(f32[16,1,4,128]{3,0,2,1:T(8,128)S(1)} %get-tuple-element.114), channel_id=1, source_target_pairs={{4,0},{8,4},{12,8},{16,12},{20,16},{24,20},{28,24},{5,1},{9,5},{13... | collective-permute-start | bytes 98312 | tf_op jit(solution)/shard_map/ppermute | solution.py:21
  97.9 6.1 %collective-permute-start.12 = (f32[16,1,4,128]{3,0,2,1:T(8,128)S(1)}, f32[16,1,4,128]{3,0,2,1:T(8,128)S(1)}, u32[]{:S(2)}, u32[]{:S(2)}) collective-permute-start(f32[16,1,4,128]{3,0,2,1:T(8,128)S(1)} %get-tuple-element.105), channel_id=1, source_target_pairs={{0,4},{4,8},{8,12},{12,16},{16,20},{20,24},{24,28},{1,5},{5,9},{9,... | collective-permute-start | bytes 98312 | tf_op jit(solution)/shard_map/ppermute | solution.py:19
  102.5 5.8 %collective-permute-start.13 = (f32[16,1,4,128]{3,0,2,1:T(8,128)S(1)}, f32[16,1,4,128]{3,0,2,1:T(8,128)S(1)}, u32[]{:S(2)}, u32[]{:S(2)}) collective-permute-start(f32[16,1,4,128]{3,0,2,1:T(8,128)S(1)} %get-tuple-element.106), channel_id=1, source_target_pairs={{4,0},{8,4},{12,8},{16,12},{20,16},{24,20},{28,24},{5,1},{9,5},{13... | collective-permute-start | bytes 98312 | tf_op jit(solution)/shard_map/ppermute | solution.py:21
  108.6 4.4 %collective-permute-start.14 = (f32[16,1,4,128]{3,0,2,1:T(8,128)S(1)}, f32[16,1,4,128]{3,0,2,1:T(8,128)S(1)}, u32[]{:S(2)}, u32[]{:S(2)}) collective-permute-start(f32[16,1,4,128]{3,0,2,1:T(8,128)S(1)} %get-tuple-element.97), channel_id=1, source_target_pairs={{0,4},{4,8},{8,12},{12,16},{16,20},{20,24},{24,28},{1,5},{5,9},{9,... | collective-permute-start | bytes 98312 | tf_op jit(solution)/shard_map/ppermute | solution.py:19
  111.5 5.8 %collective-permute-start.15 = (f32[16,1,4,128]{3,0,2,1:T(8,128)S(1)}, f32[16,1,4,128]{3,0,2,1:T(8,128)S(1)}, u32[]{:S(2)}, u32[]{:S(2)}) collective-permute-start(f32[16,1,4,128]{3,0,2,1:T(8,128)S(1)} %get-tuple-element.98), channel_id=1, source_target_pairs={{4,0},{8,4},{12,8},{16,12},{20,16},{24,20},{28,24},{5,1},{9,5},{13... | collective-permute-start | bytes 98312 | tf_op jit(solution)/shard_map/ppermute | solution.py:21
  117.4 5.8 %collective-permute-start.16 = (f32[16,1,4,128]{3,0,2,1:T(8,128)S(1)}, f32[16,1,4,128]{3,0,2,1:T(8,128)S(1)}, u32[]{:S(2)}, u32[]{:S(2)}) collective-permute-start(f32[16,1,4,128]{3,0,2,1:T(8,128)S(1)} %slice.643), channel_id=1, source_target_pairs={{4,0},{8,4},{12,8},{16,12},{20,16},{24,20},{28,24},{5,1},{9,5},{13... | collective-permute-start | bytes 98312 | tf_op jit(solution)/shard_map/ppermute | solution.py:31
  123.6 6.0 %collective-permute-start.17 = (f32[16,1,4,128]{3,0,2,1:T(8,128)S(1)}, f32[16,1,4,128]{3,0,2,1:T(8,128)S(1)}, u32[]{:S(2)}, u32[]{:S(2)}) collective-permute-start(f32[16,1,4,128]{3,0,2,1:T(8,128)S(1)} %get-tuple-element.73), channel_id=1, source_target_pairs={{0,4},{4,8},{8,12},{12,16},{16,20},{20,24},{24,28},{1,5},{5,9},{9,... | collective-permute-start | bytes 98312 | tf_op jit(solution)/shard_map/ppermute | solution.py:19
  128.0 5.8 %collective-permute-start.18 = (f32[16,1,4,128]{3,0,2,1:T(8,128)S(1)}, f32[16,1,4,128]{3,0,2,1:T(8,128)S(1)}, u32[]{:S(2)}, u32[]{:S(2)}) collective-permute-start(f32[16,1,4,128]{3,0,2,1:T(8,128)S(1)} %get-tuple-element.74), channel_id=1, source_target_pairs={{4,0},{8,4},{12,8},{16,12},{20,16},{24,20},{28,24},{5,1},{9,5},{13... | collective-permute-start | bytes 98312 | tf_op jit(solution)/shard_map/ppermute | solution.py:21
  134.2 4.5 %collective-permute-start.19 = (f32[16,1,4,128]{3,0,2,1:T(8,128)S(1)}, f32[16,1,4,128]{3,0,2,1:T(8,128)S(1)}, u32[]{:S(2)}, u32[]{:S(2)}) collective-permute-start(f32[16,1,4,128]{3,0,2,1:T(8,128)S(1)} %get-tuple-element.65), channel_id=1, source_target_pairs={{0,4},{4,8},{8,12},{12,16},{16,20},{20,24},{24,28},{1,5},{5,9},{9,... | collective-permute-start | bytes 98312 | tf_op jit(solution)/shard_map/ppermute | solution.py:19
  137.2 5.8 %collective-permute-start.20 = (f32[16,1,4,128]{3,0,2,1:T(8,128)S(1)}, f32[16,1,4,128]{3,0,2,1:T(8,128)S(1)}, u32[]{:S(2)}, u32[]{:S(2)}) collective-permute-start(f32[16,1,4,128]{3,0,2,1:T(8,128)S(1)} %get-tuple-element.66), channel_id=1, source_target_pairs={{4,0},{8,4},{12,8},{16,12},{20,16},{24,20},{28,24},{5,1},{9,5},{13... | collective-permute-start | bytes 98312 | tf_op jit(solution)/shard_map/ppermute | solution.py:21
  143.2 5.8 %collective-permute-start.21 = (f32[16,1,4,128]{3,0,2,1:T(8,128)S(1)}, f32[16,1,4,128]{3,0,2,1:T(8,128)S(1)}, u32[]{:S(2)}, u32[]{:S(2)}) collective-permute-start(f32[16,1,4,128]{3,0,2,1:T(8,128)S(1)} %slice.661), channel_id=1, source_target_pairs={{4,0},{8,4},{12,8},{16,12},{20,16},{24,20},{28,24},{5,1},{9,5},{13... | collective-permute-start | bytes 98312 | tf_op jit(solution)/shard_map/ppermute | solution.py:31
  149.5 5.3 %collective-permute-start.22 = (f32[16,1,4,128]{3,0,2,1:T(8,128)S(1)}, f32[16,1,4,128]{3,0,2,1:T(8,128)S(1)}, u32[]{:S(2)}, u32[]{:S(2)}) collective-permute-start(f32[16,1,4,128]{3,0,2,1:T(8,128)S(1)} %get-tuple-element.41), channel_id=1, source_target_pairs={{0,4},{4,8},{8,12},{12,16},{16,20},{20,24},{24,28},{1,5},{5,9},{9,... | collective-permute-start | bytes 98312 | tf_op jit(solution)/shard_map/ppermute | solution.py:19
  153.3 5.8 %collective-permute-start.23 = (f32[16,1,4,128]{3,0,2,1:T(8,128)S(1)}, f32[16,1,4,128]{3,0,2,1:T(8,128)S(1)}, u32[]{:S(2)}, u32[]{:S(2)}) collective-permute-start(f32[16,1,4,128]{3,0,2,1:T(8,128)S(1)} %get-tuple-element.42), channel_id=1, source_target_pairs={{4,0},{8,4},{12,8},{16,12},{20,16},{24,20},{28,24},{5,1},{9,5},{13... | collective-permute-start | bytes 98312 | tf_op jit(solution)/shard_map/ppermute | solution.py:21
  159.9 4.5 %collective-permute-start.24 = (f32[16,1,4,128]{3,0,2,1:T(8,128)S(1)}, f32[16,1,4,128]{3,0,2,1:T(8,128)S(1)}, u32[]{:S(2)}, u32[]{:S(2)}) collective-permute-start(f32[16,1,4,128]{3,0,2,1:T(8,128)S(1)} %get-tuple-element.33), channel_id=1, source_target_pairs={{0,4},{4,8},{8,12},{12,16},{16,20},{20,24},{24,28},{1,5},{5,9},{9,... | collective-permute-start | bytes 98312 | tf_op jit(solution)/shard_map/ppermute | solution.py:19
  162.9 5.8 %collective-permute-start.25 = (f32[16,1,4,128]{3,0,2,1:T(8,128)S(1)}, f32[16,1,4,128]{3,0,2,1:T(8,128)S(1)}, u32[]{:S(2)}, u32[]{:S(2)}) collective-permute-start(f32[16,1,4,128]{3,0,2,1:T(8,128)S(1)} %get-tuple-element.34), channel_id=1, source_target_pairs={{4,0},{8,4},{12,8},{16,12},{20,16},{24,20},{28,24},{5,1},{9,5},{13... | collective-permute-start | bytes 98312 | tf_op jit(solution)/shard_map/ppermute | solution.py:21
  169.9 6.9 %copy-start.1 = (f32[16,12,4,128]{3,0,2,1:T(8,128)S(1)}, f32[16,12,4,128]{3,0,2,1:T(8,128)}, u32[]{:S(2)}) copy-start(f32[16,12,4,128]{3,0,2,1:T(8,128)} %fusion.12) | copy-start | bytes 1179652
  172.6 17.6 %collective-permute-start.26 = (f32[16,1,4,128]{3,0,2,1:T(8,128)S(1)}, f32[16,1,4,128]{3,0,2,1:T(8,128)S(1)}, u32[]{:S(2)}, u32[]{:S(2)}) collective-permute-start(f32[16,1,4,128]{3,0,2,1:T(8,128)S(1)} %get-tuple-element.25), channel_id=1, source_target_pairs={{0,4},{4,8},{8,12},{12,16},{16,20},{20,24},{24,28},{1,5},{5,9},{9,... | collective-permute-start | bytes 98312 | tf_op jit(solution)/shard_map/ppermute | solution.py:19
  175.5 14.8 %collective-permute-start.27 = (f32[16,1,4,128]{3,0,2,1:T(8,128)S(1)}, f32[16,1,4,128]{3,0,2,1:T(8,128)S(1)}, u32[]{:S(2)}, u32[]{:S(2)}) collective-permute-start(f32[16,1,4,128]{3,0,2,1:T(8,128)S(1)} %get-tuple-element.26), channel_id=1, source_target_pairs={{4,0},{8,4},{12,8},{16,12},{20,16},{24,20},{28,24},{5,1},{9,5},{13... | collective-permute-start | bytes 98312 | tf_op jit(solution)/shard_map/ppermute | solution.py:21
  187.3 2.9 %copy-start.2 = (f32[64,12,4,128]{3,0,2,1:T(8,128)S(1)}, f32[64,12,4,128]{3,0,2,1:T(8,128)}, u32[]{:S(2)}) copy-start(f32[64,12,4,128]{3,0,2,1:T(8,128)} %all-gather.2.cloned.1.call-done) | copy-start | bytes 4718596
Sparse Core Ops, SparseCore 0:
  170.0 17.2 all-gather.1
where the time goes:
time: 237 us; the launch traced here: 236 us
  waiting for transfers between devices  72.6 us (31%)
  starting transfers between devices  71.1 us (30%)
  blocking collectives  37.1 us (16%)
  local copies, waits for them, and re-layouts  29.9 us (13%)
  between operations  14.9 us (6%)
  other arithmetic  6.3 us (3%)
  matrix products  4.36 us (2%)
    ppermute x12, waiting for transfers between devices, with_halo(): lax.ppermute(head, axis, [((i + 1) % count, i) for i in range(ends)])  47.9 us
    ppermute x12, starting transfers between devices, with_halo(): lax.ppermute(tail, axis, [(i, (i + 1) % count) for i in range(ends)])  46.7 us
    psum x1, blocking collectives, local(): gram_rows, cross_rows = lax.psum((gram_block, cross_block), 'slab')  37.1 us
    gather x2, local copies, waits for them, and re-layouts, local(): loads = jnp.take(case_rows, panel, axis=1) * span * keep  23.3 us
    ppermute x12, starting transfers between devices, with_halo(): lax.ppermute(head, axis, [((i + 1) % count, i) for i in range(ends)])  15.5 us
    ppermute x4, waiting for transfers between devices, from_behind(): return lax.ppermute(x, axis, pairs)  12 us
    all_gather x1, waiting for transfers between devices, local(): piece = lax.all_gather(fields, 'case', axis=0, tiled=True)  10.2 us
    ppermute x4, starting transfers between devices, from_behind(): return lax.ppermute(x, axis, pairs)  8.95 us
  transfers between devices with their start and end apart: 29, of which 26 were waited for; matrix products, arithmetic and copies ran while one was open for 3% of the time, Pallas kernels for 0%

commit v1 on v0

v1 whole, which is shorter than its diff:
```python
import functools

import jax
import jax.numpy as jnp
from jax import lax
from jax.experimental import pallas as pl
from jax.experimental.pallas import tpu as pltpu
from jax.sharding import PartitionSpec as P

damping = 0.7
penalty = 4.0
f32 = jnp.float32
bf16 = jnp.bfloat16
SUB = 8
REACH = 32
BELOW, ABOVE = 29, 30


def over(lo, hi, step, body):
    count = hi - lo + 1
    whole = count // step
    if whole > 1:

        def trip(i, carry):
            body(lo + i * step, step)
            return carry

        lax.fori_loop(0, whole, trip, 0)
    elif whole == 1:
        body(lo, step)
    if count - whole * step:
        body(lo + whole * step, count - whole * step)


def cycle_kernel(
    meta, table, panel, flags, diagonal, *refs, tiles, own_tiles, n, total, R, hops
):
    mine, theirs = refs[:hops], refs[hops : 2 * hops]
    field_out, all_out, left_out = refs[2 * hops : 2 * hops + 3]
    ext, low, high, scale, w0, d0, w1, d1, w2, b0, va, vb, b1, xa, xb, b2, ya, yb, kept = refs[2 * hops + 3 :]
    base = meta[0] * n - REACH
    even_group = meta[1] == 0
    own_slot = meta[2]
    lanes = table.shape[-1]
    quads = table.shape[0] // tiles
    per = SUB // R

    near = n // per
    for which, own in enumerate((panel, flags, diagonal)):
        ext[which, pl.ds(REACH // per, near)] = own[...].astype(f32)
    for k in range(1, hops + 1):
        depth = min(n, REACH - (k - 1) * n) // per
        below = (REACH - (k - 1) * n) // per - depth
        above = (REACH + k * n) // per
        for which in range(3):
            first, last = pl.ds(0, depth), pl.ds(near - depth, depth)
            ext[which, pl.ds(below, depth)] = jnp.where(even_group, mine[k - 1][which, last], theirs[k - 1][which, last])
            ext[which, pl.ds(above, depth)] = jnp.where(even_group, theirs[k - 1][which, first], mine[k - 1][which, first])

    shape = ext.shape[1:]
    position = lax.broadcasted_iota(jnp.int32, shape, 0) * per + lax.broadcasted_iota(jnp.int32, shape, 1) // R + base
    inside = (position >= 0) & (position < total)
    held = ext[1]
    coeff = ext[2] + penalty * held
    span = 1.0 + 2.0 * position.astype(f32) / total
    scale[...] = jnp.where(inside, span * (1.0 - held), 0.0).reshape(scale.shape)
    index = ext[0].astype(jnp.int32)
    low[...] = (index % lanes).reshape(low.shape)
    high[...] = (index // lanes).reshape(high.shape)
    d = coeff + 6.0
    d0[...] = d.reshape(d0.shape)
    w0[...] = jnp.where(inside, damping / d, 0.0).reshape(w0.shape)
    coeff = 0.5 * (coeff + pltpu.roll(coeff, R, 1))
    position = lax.broadcasted_iota(jnp.int32, shape, 0) + base // 2
    d = coeff + 4.5
    d1[...] = d.reshape(d1.shape)
    w1[...] = jnp.where((position >= 0) & (position < total // 2), damping / d, 0.0).reshape(w1.shape)
    coeff = coeff.reshape(shape[0] // 2, 2, *shape[1:])
    coeff = 0.5 * (coeff[:, 0] + coeff[:, 1])
    position = lax.broadcasted_iota(jnp.int32, coeff.shape, 0) + base // 4
    w2[...] = jnp.where((position >= 0) & (position < total // 4), damping / (coeff + 4.125), 0.0).reshape(w2.shape)

    def node(ref, layer, r, fine):
        return ref[pl.ds(layer * (R if fine else SUB) + r, 1), :]

    def rows(ref, layer, t):
        return [ref[layer * R + r, pl.ds(t * SUB, SUB), :] for r in range(R)]

    def put(ref, layer, t, values):
        for r in range(R):
            ref[layer * R + r, pl.ds(t * SUB, SUB), :] = values[r]

    def around(below, here, above, weight):
        out = []
        for r in range(R):
            axial = below[r] + above[r]
            if weight != 1.0:
                axial = weight * axial
            side = pltpu.roll(here[r], 1, 1) + pltpu.roll(here[r], lanes - 1, 1)
            if r > 0:
                side = side + here[r - 1]
            if r < R - 1:
                side = side + here[r + 1]
            out.append(axial + side)
        return out

    def sweep(src, dst, b, w, lo, hi, weight, fine, step=8):
        def body(layer, count):
            for t in range(tiles):
                v = [rows(src, layer + i - 1, t) for i in range(count + 2)]
                new = []
                for i in range(count):
                    nv = around(v[i], v[i + 1], v[i + 2], weight)
                    bb = rows(b, layer + i, t)
                    new.append([(1.0 - damping) * v[i + 1][r] + node(w, layer + i, r, fine) * (bb[r] + nv[r]) for r in range(R)])
                for i in range(count):
                    put(dst, layer + i, t, new[i])

        over(lo, hi, step, body)

    def loads(layer, count):
        for i in range(count):
            for r in range(R):
                lo = jnp.broadcast_to(node(low, layer + i, r, True), (SUB, lanes))
                hi = jnp.broadcast_to(node(high, layer + i, r, True), (SUB, lanes))
                factor = node(scale, layer + i, r, True)
                w = node(w0, layer + i, r, True)
                at = [hi == q for q in range(quads)]
                for t in range(tiles):
                    value = jnp.take_along_axis(table[t * quads], lo, axis=1)
                    for q in range(1, quads):
                        value = jnp.where(at[q], jnp.take_along_axis(table[t * quads + q], lo, axis=1), value)
                    value = value * factor
                    b0[(layer + i) * R + r, pl.ds(t * SUB, SUB), :] = value
                    va[(layer + i) * R + r, pl.ds(t * SUB, SUB), :] = value * w

    def residual(src, b, d, layer, t, weight, fine):
        v = [rows(src, layer + i - 1, t) for i in range(3)]
        nv = around(v[0], v[1], v[2], weight)
        bb = rows(b, layer, t)
        return [bb[r] - node(d, layer, r, fine) * v[1][r] + nv[r] for r in range(R)]

    def restrict(src, b, d, weight, fine, coarse_b, coarse_v, w, lo, hi, start, step):
        for t in range(tiles):
            put(kept, 0, t, residual(src, b, d, 2 * lo - 1, t, weight, fine))

        def body(layer, count):
            for t in range(tiles):
                before = rows(kept, 0, t)
                got = []
                for i in range(count):
                    even = residual(src, b, d, 2 * (layer + i), t, weight, fine)
                    odd = residual(src, b, d, 2 * (layer + i) + 1, t, weight, fine)
                    lead = jnp.where(layer + i + start > 0, 0.25, 0.0).astype(f32)
                    got.append([0.5 * even[r] + (0.25 * odd[r] + lead * before[r]) for r in range(R)])
                    before = odd
                put(kept, 0, t, before)
                for i in range(count):
                    put(coarse_b, layer + i, t, got[i])
                    put(coarse_v, layer + i, t, [got[i][r] * node(w, layer + i, r, False) for r in range(R)])

        over(lo, hi, step, body)

    def prolong(coarse, fine, lo, hi, start, step=4):
        def body(layer, count):
            for t in range(tiles):
                c = [rows(coarse, layer + i, t) for i in range(count + 1)]
                for i in range(count):
                    half = jnp.where(layer + i + start >= 0, 0.5, 0.0).astype(f32)
                    v = rows(fine, 2 * (layer + i), t)
                    put(fine, 2 * (layer + i), t, [v[r] + c[i][r] for r in range(R)])
                    v = rows(fine, 2 * (layer + i) + 1, t)
                    put(fine, 2 * (layer + i) + 1, t, [v[r] + half * (c[i][r] + c[i + 1][r]) for r in range(R)])

        over(lo, hi, step, body)

    first, last = REACH - BELOW, REACH + n - 1 + ABOVE
    over(first, last, 4, loads)
    sweep(va, vb, b0, w0, first + 1, last - 1, 1.0, True)
    mid, half = REACH // 2, n // 2
    restrict(vb, b0, d0, 1.0, True, b1, xa, w1, mid - 13, mid + half + 13, base // 2, 5)
    sweep(xa, xb, b1, w1, mid - 12, mid + half + 12, 0.25, False)
    low_mid, quarter = REACH // 4, n // 4
    restrict(xb, b1, d1, 0.25, False, b2, ya, w2, low_mid - 5, low_mid + quarter + 5, base // 4, 4)
    sweep(ya, yb, b2, w2, low_mid - 4, low_mid + quarter + 4, 0.0625, False)
    sweep(yb, ya, b2, w2, low_mid - 3, low_mid + quarter + 3, 0.0625, False)
    sweep(ya, yb, b2, w2, low_mid - 2, low_mid + quarter + 2, 0.0625, False)
    prolong(yb, xb, low_mid - 2, low_mid + quarter + 1, base // 4)
    sweep(xb, xa, b1, w1, mid - 3, mid + half + 2, 0.25, False)
    sweep(xa, xb, b1, w1, mid - 2, mid + half + 1, 0.25, False)
    prolong(xb, vb, mid - 2, mid + half + 1, base // 2)
    sweep(vb, va, b0, w0, REACH - 2, REACH + n + 1, 1.0, True)
    sweep(va, vb, b0, w0, REACH - 1, REACH + n, 1.0, True)

    def finish(layer, count):
        for i in range(count):
            for r in range(R):
                all_out[(layer + i - REACH) * R + r] = vb[(layer + i) * R + r]
        for t in range(own_tiles):
            tile = own_slot * own_tiles + t

            def at(ref, e, r):
                return ref[e * R + r, pl.ds(pl.multiple_of(tile * SUB, SUB), SUB), :]

            v = [[at(vb, layer + i - 1, r) for r in range(R)] for i in range(count + 2)]
            for i in range(count):
                nv = around(v[i], v[i + 1], v[i + 2], 1.0)
                for r in range(R):
                    row = (layer + i - REACH) * R + r
                    field_out[pl.ds(t * SUB, SUB), row, :] = v[i + 1][r]
                    left_out[row, pl.ds(t * SUB, SUB), :] = node(d0, layer + i, r, True) * v[i + 1][r] - nv[r]
                    left_out[row, pl.ds((own_tiles + t) * SUB, SUB), :] = at(b0, layer + i, r)

    over(REACH, REACH + n - 1, 4, finish)


def cycle(meta, table, panel, flags, diagonal, mine, theirs, cases, own, n, total, R):
    hops = len(mine)
    extent = n + 2 * REACH
    lanes = table.shape[2]

    def field(layers):
        return pltpu.VMEM((layers * R, cases, lanes), f32)

    def coefficients(rows, dtype=f32):
        return pltpu.VMEM((rows, lanes), dtype)

    fine, middle, coarse = extent * R, extent // 2 * SUB, extent // 4 * SUB
    scratch = [
        pltpu.VMEM((3, fine // SUB, SUB, lanes), f32),
        coefficients(fine, jnp.int32),
        coefficients(fine, jnp.int32),
        *(coefficients(rows) for rows in (fine, fine, fine, middle, middle, coarse)),
        *(field(extent) for _ in range(3)),
        *(field(extent // 2) for _ in range(3)),
        *(field(extent // 4) for _ in range(3)),
        field(1),
    ]
    vmem = pl.BlockSpec(memory_space=pltpu.VMEM)
    return pl.pallas_call(
        functools.partial(cycle_kernel, tiles=cases // SUB, own_tiles=own // SUB, n=n, total=total, R=R, hops=hops),
        out_shape=(
            jax.ShapeDtypeStruct((own, n * R, lanes), f32),
            jax.ShapeDtypeStruct((n * R, cases, lanes), f32),
            jax.ShapeDtypeStruct((n * R, 2 * own, lanes), f32),
        ),
        in_specs=[pl.BlockSpec(memory_space=pltpu.SMEM)] + [vmem] * (4 + 2 * hops),
        out_specs=[vmem] * 3,
        scratch_shapes=scratch,
        compiler_params=pltpu.CompilerParams(vmem_limit_bytes=48 * 2**20),
    )(meta, table, panel, flags, diagonal, *mine, *theirs)


def gram_kernel(meta, left, here, there, out, *, own):
    even_group = meta[1] == 0
    rows, cases, lanes = here.shape
    slots = cases // own

    def halves(x):
        top = x.astype(bf16)
        return top, (x - top.astype(f32)).astype(bf16)

    def dot(a, b):
        return lax.dot_general(a, b, (((1,), (1,)), ((), ())), preferred_element_type=f32)

    together = 4

    def trip(i, total):
        a = jnp.concatenate([left[i * together + j] for j in range(together)], axis=1)
        h = jnp.concatenate([here[i * together + j] for j in range(together)], axis=1)
        o = jnp.concatenate([there[i * together + j] for j in range(together)], axis=1)
        even, odd = jnp.where(even_group, h, o), jnp.where(even_group, o, h)
        parts = []
        for q in range(slots):
            parts += [even[q * own : (q + 1) * own], odd[q * own : (q + 1) * own]]
        b = jnp.concatenate(parts, axis=0)
        a_top, a_rest = halves(a)
        b_top, b_rest = halves(b)
        return total + (dot(a_top, b_top) + (dot(a_top, b_rest) + dot(a_rest, b_top)))

    out[...] = lax.fori_loop(0, rows // together, trip, jnp.zeros(out.shape, f32))


def products(meta, left, here, there, own):
    vmem = pl.BlockSpec(memory_space=pltpu.VMEM)
    return pl.pallas_call(
        functools.partial(gram_kernel, own=own),
        out_shape=jax.ShapeDtypeStruct((left.shape[1], 2 * here.shape[1]), f32),
        in_specs=[pl.BlockSpec(memory_space=pltpu.SMEM)] + [vmem] * 3,
        out_specs=vmem,
        compiler_params=pltpu.CompilerParams(vmem_limit_bytes=32 * 2**20),
    )(meta, left, here, there)


def sum_over_slabs(x):
    count = lax.axis_size("slab")
    if count & (count - 1):
        return lax.psum(x, "slab")
    by = 1
    while by < count:
        x = x + lax.ppermute(x, "slab", [(i, i ^ by) for i in range(count)])
        by *= 2
    return x


def local(pressure, panel, flags, diagonal):
    n, R, lanes = panel.shape
    slabs, groups = lax.axis_size("slab"), lax.axis_size("case")
    own = pressure.shape[0] // groups
    slots = groups // 2
    cases = own * slots
    total = n * slabs
    slab, group = lax.axis_index("slab"), lax.axis_index("case")
    meta = jnp.stack([slab, group % 2, group // 2]).astype(jnp.int32)

    per = SUB // R
    packed = [x.reshape(n // per, SUB, lanes) for x in (panel, flags, diagonal)]
    block = jnp.stack([x.astype(f32) for x in packed])
    hops = -(-REACH // n)
    mine = []
    for k in range(1, hops + 1):
        pairs = []
        for s in range(slabs):
            for g in range(groups):
                source = (s - k if g % 2 == 0 else s + k) % slabs
                pairs.append((source * groups + g, s * groups + g))
        mine.append(lax.ppermute(block, ("slab", "case"), pairs))
    swap = [(g, g ^ 1) for g in range(groups)]
    theirs = [lax.ppermute(x, "case", swap) for x in mine]

    table = pressure.reshape(slots, 2, own // SUB, SUB, -1, lanes)
    table = lax.dynamic_index_in_dim(table, group % 2, 1, keepdims=False)
    table = table.swapaxes(2, 3).reshape(-1, SUB, lanes)

    fields, worked, left = cycle(meta, table, *packed, mine, theirs, cases, own, n, total, R)
    received = lax.ppermute(worked, "case", swap)
    sums = sum_over_slabs(products(meta, left, worked, received, own))
    sums = sums * (1.0 / (total * R * lanes))
    return fields.reshape(own, n, R, lanes), sums[:own], sums[own:]


def solution(mesh):
    in_specs = (P(), P("slab", None, None), P("slab", None, None), P("slab", None, None))
    out_specs = (P("case", "slab", None, None), P("case", None), P("case", None))
    return jax.shard_map(local, mesh=mesh, in_specs=in_specs, out_specs=out_specs, check_vma=False)
```

time: 237 us -> 55.3 us (0.23)
  starting transfers between devices: 71.1 us -> 8.72 us
  waiting for transfers between devices: 72.6 us -> 19.5 us
  blocking collectives: 37.1 us -> 0 us
  local copies, waits for them, and re-layouts: 29.9 us -> 1.35 us
  Pallas kernels: 0 us -> 23.9 us
  between operations: 14.9 us -> 0.7 us
  other arithmetic: 6.3 us -> 0.89 us
  matrix products: 4.36 us -> 0 us
    ppermute x28 -> x10, starting transfers between devices: 71.1 us -> 8.72 us  [the longest x3 7.08 us: local(): mine.append(lax.ppermute(block, ('slab', 'case'), pairs))]
    ppermute x28 -> x10, waiting for transfers between devices: 62.4 us -> 19.5 us  [the longest x3 10.7 us: sum_over_slabs(): x = x + lax.ppermute(x, 'slab', [(i, i ^ by) for i in range(count)])]
    psum x1 -> x0, blocking collectives: 37.1 us -> none  [local(): gram_rows, cross_rows = lax.psum((gram_block, cross_block), 'slab')]
    pallas_call x0 -> x2, Pallas kernels: none -> 23.9 us  [the longest x1 21.1 us: cycle(): pl.pallas_call(functools.partial(cycle_kernel, tiles=cases // SUB, own_ti...]
    gather x2 -> x0, local copies, waits for them, and re-layouts: 23.3 us -> none  [local(): loads = jnp.take(case_rows, panel, axis=1) * span * keep]
    all_gather x1 -> x0, waiting for transfers between devices: 10.2 us -> none  [local(): piece = lax.all_gather(fields, 'case', axis=0, tiled=True)]
    dot_general x2 -> x0, matrix products: 4.36 us -> none  [the longest x1 2.91 us: local(): lax.dot_general(loads_flat, piece_flat, contract, precision=highest, pref...]
    slice x58 -> x1, local copies, waits for them, and re-layouts: 4.52 us -> 0.61 us  [local(): return (fields.reshape(own, n, R, lanes), sums[:own], sums[own:])]
  transfers between devices with their start and end apart: 29 -> 10, of which waited for: 26 -> 8; matrix products, arithmetic and copies ran while one was open for 3% -> 0% of each run, Pallas kernels for 0% -> 0%
where the time goes in v1:
time: 55.3 us; the launch traced here: 55.1 us
  Pallas kernels  23.9 us (43%)
  waiting for transfers between devices  19.5 us (35%)
  starting transfers between devices  8.72 us (16%)
  local copies, waits for them, and re-layouts  1.35 us (2%)
  other arithmetic  0.89 us (2%)
  between operations  0.7 us (1%)
    pallas_call x1, Pallas kernels, cycle(): pl.pallas_call(functools.partial(cycle_kernel, tiles=cases // SUB, own_ti...  21.1 us
    ppermute x3, waiting for transfers between devices, sum_over_slabs(): x = x + lax.ppermute(x, 'slab', [(i, i ^ by) for i in range(count)])  10.7 us
    ppermute x3, starting transfers between devices, local(): mine.append(lax.ppermute(block, ('slab', 'case'), pairs))  7.08 us
    ppermute x3, waiting for transfers between devices, local(): mine.append(lax.ppermute(block, ('slab', 'case'), pairs))  5.51 us
    pallas_call x1, Pallas kernels, products(): pl.pallas_call(functools.partial(gram_kernel, own=own), out_shape=jax.Sha...  2.82 us
    ppermute x1, waiting for transfers between devices, local(): received = lax.ppermute(worked, 'case', swap)  2.13 us
    ppermute x3, starting transfers between devices, sum_over_slabs(): x = x + lax.ppermute(x, 'slab', [(i, i ^ by) for i in range(count)])  1.48 us
    ppermute x3, waiting for transfers between devices, local(): theirs = [lax.ppermute(x, 'case', swap) for x in mine]  1.19 us
  transfers between devices with their start and end apart: 10, of which 8 were waited for; matrix products, arithmetic and copies ran while one was open for 0% of the time, Pallas kernels for 0%

profile of v1, /device:TPU:0, one launch (start us, length us, event | category | flops | bytes accessed | tf_op | source)
XLA Modules:
  0.0 55.1 jit_solution(4231800965326799032)
XLA Ops:
  0.6 0.0 copy-start
  0.6 0.0 copy-start.3
  0.7 0.8 %convert_element_type.26 = f32[12,4,128]{2,1,0:T(4,128)S(1)} convert(s32[12,4,128]{2,1,0:T(4,128)} %param.5) | non-fusion elementwise | flops 6144 | bytes 49152 | tf_op jit(solution)/shard_map/convert_element_type | solution.py:318
  1.4 0.0 copy-done.3
  1.4 0.0 copy-start.1
  1.5 0.7 %copy-done.1 = f32[12,4,128]{2,1,0:T(4,128)S(1)} copy-done((f32[12,4,128]{2,1,0:T(4,128)S(1)}, f32[12,4,128]{2,1,0:T(4,128)}, u32[]{:S(2)}) %copy-start.1) | copy-done | bytes 24600
  2.2 4.0 %collective-permute-start.2 = (f32[3,6,8,128]{3,2,1,0:T(8,128)S(1)}, f32[3,6,8,128]{3,2,1,0:T(8,128)S(1)}, u32[]{:S(2)}, u32[]{:S(2)}) collective-permute-start(f32[3,6,8,128]{3,2,1,0:T(8,128)S(1)} %pad_maximum_fusion), channel_id=1, source_target_pairs={{20,0},{13,1},{22,2},{15,3},{24,4},{17,5},{26,6},{19,7},{28,8},{21... | collective-permute-start | bytes 221192 | tf_op jit(solution)/shard_map/ppermute | solution.py:327
  6.2 1.6 %collective-permute-start.1 = (f32[3,6,8,128]{3,2,1,0:T(8,128)S(1)}, f32[3,6,8,128]{3,2,1,0:T(8,128)S(1)}, u32[]{:S(2)}, u32[]{:S(2)}) collective-permute-start(f32[3,6,8,128]{3,2,1,0:T(8,128)S(1)} %pad_maximum_fusion), channel_id=1, source_target_pairs={{24,0},{9,1},{26,2},{11,3},{28,4},{13,5},{30,6},{15,7},{0,8},{17,9... | collective-permute-start | bytes 221192 | tf_op jit(solution)/shard_map/ppermute | solution.py:327
  7.7 1.5 %collective-permute-start = (f32[3,6,8,128]{3,2,1,0:T(8,128)S(1)}, f32[3,6,8,128]{3,2,1,0:T(8,128)S(1)}, u32[]{:S(2)}, u32[]{:S(2)}) collective-permute-start(f32[3,6,8,128]{3,2,1,0:T(8,128)S(1)} %pad_maximum_fusion), channel_id=1, source_target_pairs={{28,0},{5,1},{30,2},{7,3},{0,4},{9,5},{2,6},{11,7},{4,8},{13,9},{6... | collective-permute-start | bytes 221192 | tf_op jit(solution)/shard_map/ppermute | solution.py:327
  9.3 0.0 copy-done
  9.3 0.0 copy-start.2
  9.3 1.2 %collective-permute-done.2.refs_2_ = f32[3,6,8,128]{3,2,1,0:T(8,128)S(1)} collective-permute-done((f32[3,6,8,128]{3,2,1,0:T(8,128)S(1)}, f32[3,6,8,128]{3,2,1,0:T(8,128)S(1)}, u32[]{:S(2)}, u32[]{:S(2)}) %collective-permute-start.2) | collective-permute-done | bytes 73760 | tf_op jit(solution)/shard_map/ppermute | solution.py:327
  10.5 0.0 collective-permute-start.5
  10.5 2.5 %collective-permute-done.1.refs_1_ = f32[3,6,8,128]{3,2,1,0:T(8,128)S(1)} collective-permute-done((f32[3,6,8,128]{3,2,1,0:T(8,128)S(1)}, f32[3,6,8,128]{3,2,1,0:T(8,128)S(1)}, u32[]{:S(2)}, u32[]{:S(2)}) %collective-permute-start.1) | collective-permute-done | bytes 73760 | tf_op jit(solution)/shard_map/ppermute | solution.py:327
  13.0 0.0 collective-permute-start.4
  13.0 1.8 %collective-permute-done.refs_0_ = f32[3,6,8,128]{3,2,1,0:T(8,128)S(1)} collective-permute-done((f32[3,6,8,128]{3,2,1,0:T(8,128)S(1)}, f32[3,6,8,128]{3,2,1,0:T(8,128)S(1)}, u32[]{:S(2)}, u32[]{:S(2)}) %collective-permute-start) | collective-permute-done | bytes 73760 | tf_op jit(solution)/shard_map/ppermute | solution.py:327
  14.8 0.0 collective-permute-start.3
  14.8 0.1 pad_add_fusion.meta
  14.9 0.0 collective-permute-done.5.refs_5_
  14.9 0.0 collective-permute-done.4.refs_4_
  14.9 1.2 %collective-permute-done.3.refs_3_ = f32[3,6,8,128]{3,2,1,0:T(8,128)S(1)} collective-permute-done((f32[3,6,8,128]{3,2,1,0:T(8,128)S(1)}, f32[3,6,8,128]{3,2,1,0:T(8,128)S(1)}, u32[]{:S(2)}, u32[]{:S(2)}) %collective-permute-start.3) | collective-permute-done | bytes 73760 | tf_op jit(solution)/shard_map/ppermute | solution.py:329
  16.1 0.0 copy-done.2
  16.1 21.1 %shard_map.67 = (f32[16,48,128]{2,1,0:T(8,128)}, f32[48,32,128]{2,1,0:T(8,128)S(1)}, f32[48,32,128]{2,1,0:T(8,128)S(1)}) custom-call(s32[3]{0:T(128)S(1)} %pad_add_fusion.meta, f32[16,8,128]{2,1,0:T(8,128)S(1)} %bitcast.17, s32[6,8,128]{2,1,0:T(8,128)S(1)} %bitcast.20, s32[6,8,128]{2,1,0:T(8,128)S(1)} %bitcast.21, f32[6,8,128]{2,1,0:T(8,128)S(1)} %bitcast.19, ...), custom_call_target="tpu_custom_call" | custom-call | tf_op jit(solution)/shard_map/pallas_call | solution.py:240
  37.2 0.2 collective-permute-start.6
  37.3 2.1 %collective-permute-done.6.there = f32[48,32,128]{2,1,0:T(8,128)S(1)} collective-permute-done((f32[48,32,128]{2,1,0:T(8,128)S(1)}, f32[48,32,128]{2,1,0:T(8,128)S(1)}, u32[]{:S(2)}, u32[]{:S(2)}) %collective-permute-start.6) | collective-permute-done | bytes 786464 | tf_op jit(solution)/shard_map/ppermute | solution.py:336
  39.5 2.8 %shard_map.68 = f32[32,64]{1,0:T(8,128)S(1)} custom-call(s32[3]{0:T(128)S(1)} %pad_add_fusion.meta, f32[48,32,128]{2,1,0:T(8,128)S(1)} %get-tuple-element.7.left, f32[48,32,128]{2,1,0:T(8,128)S(1)} %get-tuple-element.8.here, f32[48,32,128]{2,1,0:T(8,128)S(1)} %collective-permute-done.6.there), custom_call_target="tpu_custom_call" | custom-call | tf_op jit(solution)/shard_map/pallas_call | solution.py:286
  42.3 0.1 collective-permute-start.7
  42.4 3.7 %collective-permute-done.7 = f32[32,64]{1,0:T(8,128)S(1)} collective-permute-done((f32[32,64]{1,0:T(8,128)S(1)}, f32[32,64]{1,0:T(8,128)S(1)}, u32[]{:S(2)}, u32[]{:S(2)}) %collective-permute-start.7) | collective-permute-done | bytes 8224 | tf_op jit(solution)/shard_map/ppermute | solution.py:301
  46.1 0.0 collective-permute-start.8
  46.1 3.7 %collective-permute-done.8 = f32[32,64]{1,0:T(8,128)S(1)} collective-permute-done((f32[32,64]{1,0:T(8,128)S(1)}, f32[32,64]{1,0:T(8,128)S(1)}, u32[]{:S(2)}, u32[]{:S(2)}) %collective-permute-start.8) | collective-permute-done | bytes 8224 | tf_op jit(solution)/shard_map/ppermute | solution.py:301
  49.8 1.4 %collective-permute-start.9 = (f32[32,64]{1,0:T(8,128)S(1)}, f32[32,64]{1,0:T(8,128)S(1)}, u32[]{:S(2)}, u32[]{:S(2)}) collective-permute-start(f32[32,64]{1,0:T(8,128)S(1)} %add.22), channel_id=1, source_target_pairs={{0,16},{4,20},{8,24},{12,28},{16,0},{20,4},{24,8},{28,12},{1,17},{... | collective-permute-start | bytes 24584 | tf_op jit(solution)/shard_map/ppermute | solution.py:301
  51.2 3.2 %collective-permute-done.9 = f32[32,64]{1,0:T(8,128)S(1)} collective-permute-done((f32[32,64]{1,0:T(8,128)S(1)}, f32[32,64]{1,0:T(8,128)S(1)}, u32[]{:S(2)}, u32[]{:S(2)}) %collective-permute-start.9) | collective-permute-done | bytes 8224 | tf_op jit(solution)/shard_map/ppermute | solution.py:301
  54.5 0.6 %fusion = (f32[16,64]{1,0:T(8,128)}, f32[16,64]{1,0:T(8,128)}) fusion(f32[32,64]{1,0:T(8,128)S(1)} %add_multiply_fusion), kind=kLoop, calls=%fused_computation.4 | loop fusion | bytes 16384 | tf_op jit(solution)/shard_map/slice | solution.py:339
  (6 shorter events, 0.0 us)
Async XLA Ops:
  0.6 8.6 %copy-start = (f32[64,512]{1,0:T(8,128)S(1)}, f32[64,512]{1,0:T(8,128)}, u32[]{:S(2)}) copy-start(f32[64,512]{1,0:T(8,128)} %param.4) | copy-start | bytes 393220
  0.6 0.8 %copy-start.3 = (s32[12,4,128]{2,1,0:T(4,128)S(1)}, s32[12,4,128]{2,1,0:T(4,128)}, u32[]{:S(2)}) copy-start(s32[12,4,128]{2,1,0:T(4,128)} %param.6) | copy-start | bytes 73732
  1.4 0.7 %copy-start.1 = (f32[12,4,128]{2,1,0:T(4,128)S(1)}, f32[12,4,128]{2,1,0:T(4,128)}, u32[]{:S(2)}) copy-start(f32[12,4,128]{2,1,0:T(4,128)} %param.7) | copy-start | bytes 73732
  2.2 8.3 %collective-permute-start.2 = (f32[3,6,8,128]{3,2,1,0:T(8,128)S(1)}, f32[3,6,8,128]{3,2,1,0:T(8,128)S(1)}, u32[]{:S(2)}, u32[]{:S(2)}) collective-permute-start(f32[3,6,8,128]{3,2,1,0:T(8,128)S(1)} %pad_maximum_fusion), channel_id=1, source_target_pairs={{20,0},{13,1},{22,2},{15,3},{24,4},{17,5},{26,6},{19,7},{28,8},{21... | collective-permute-start | bytes 221192 | tf_op jit(solution)/shard_map/ppermute | solution.py:327
  6.2 6.8 %collective-permute-start.1 = (f32[3,6,8,128]{3,2,1,0:T(8,128)S(1)}, f32[3,6,8,128]{3,2,1,0:T(8,128)S(1)}, u32[]{:S(2)}, u32[]{:S(2)}) collective-permute-start(f32[3,6,8,128]{3,2,1,0:T(8,128)S(1)} %pad_maximum_fusion), channel_id=1, source_target_pairs={{24,0},{9,1},{26,2},{11,3},{28,4},{13,5},{30,6},{15,7},{0,8},{17,9... | collective-permute-start | bytes 221192 | tf_op jit(solution)/shard_map/ppermute | solution.py:327
  7.7 7.0 %collective-permute-start = (f32[3,6,8,128]{3,2,1,0:T(8,128)S(1)}, f32[3,6,8,128]{3,2,1,0:T(8,128)S(1)}, u32[]{:S(2)}, u32[]{:S(2)}) collective-permute-start(f32[3,6,8,128]{3,2,1,0:T(8,128)S(1)} %pad_maximum_fusion), channel_id=1, source_target_pairs={{28,0},{5,1},{30,2},{7,3},{0,4},{9,5},{2,6},{11,7},{4,8},{13,9},{6... | collective-permute-start | bytes 221192 | tf_op jit(solution)/shard_map/ppermute | solution.py:327
  9.3 6.8 %copy-start.2 = (s32[12,4,128]{2,1,0:T(4,128)S(1)}, s32[12,4,128]{2,1,0:T(4,128)}, u32[]{:S(2)}) copy-start(s32[12,4,128]{2,1,0:T(4,128)} %param.5) | copy-start | bytes 73732
  10.5 4.4 %collective-permute-start.5 = (f32[3,6,8,128]{3,2,1,0:T(8,128)S(1)}, f32[3,6,8,128]{3,2,1,0:T(8,128)S(1)}, u32[]{:S(2)}, u32[]{:S(2)}) collective-permute-start(f32[3,6,8,128]{3,2,1,0:T(8,128)S(1)} %collective-permute-done.2.refs_2_), channel_id=1, source_target_pairs={{0,1},{1,0},{2,3},{3,2},{4,5},{5,4},{6,7},{7,6},{8,9},{9,8},{10,11... | collective-permute-start | bytes 221192 | tf_op jit(solution)/shard_map/ppermute | solution.py:329
  13.0 1.9 %collective-permute-start.4 = (f32[3,6,8,128]{3,2,1,0:T(8,128)S(1)}, f32[3,6,8,128]{3,2,1,0:T(8,128)S(1)}, u32[]{:S(2)}, u32[]{:S(2)}) collective-permute-start(f32[3,6,8,128]{3,2,1,0:T(8,128)S(1)} %collective-permute-done.1.refs_1_), channel_id=1, source_target_pairs={{0,1},{1,0},{2,3},{3,2},{4,5},{5,4},{6,7},{7,6},{8,9},{9,8},{10,11... | collective-permute-start | bytes 221192 | tf_op jit(solution)/shard_map/ppermute | solution.py:329
  14.8 1.3 %collective-permute-start.3 = (f32[3,6,8,128]{3,2,1,0:T(8,128)S(1)}, f32[3,6,8,128]{3,2,1,0:T(8,128)S(1)}, u32[]{:S(2)}, u32[]{:S(2)}) collective-permute-start(f32[3,6,8,128]{3,2,1,0:T(8,128)S(1)} %collective-permute-done.refs_0_), channel_id=1, source_target_pairs={{0,1},{1,0},{2,3},{3,2},{4,5},{5,4},{6,7},{7,6},{8,9},{9,8},{10,11... | collective-permute-start | bytes 221192 | tf_op jit(solution)/shard_map/ppermute | solution.py:329
  37.2 2.3 %collective-permute-start.6 = (f32[48,32,128]{2,1,0:T(8,128)S(1)}, f32[48,32,128]{2,1,0:T(8,128)S(1)}, u32[]{:S(2)}, u32[]{:S(2)}) collective-permute-start(f32[48,32,128]{2,1,0:T(8,128)S(1)} %get-tuple-element.8.here), channel_id=1, source_target_pairs={{0,1},{1,0},{2,3},{3,2},{4,5},{5,4},{6,7},{7,6},{8,9},{9,8},{10,11... | collective-permute-start | bytes 2359304 | tf_op jit(solution)/shard_map/ppermute | solution.py:336
  42.3 3.8 %collective-permute-start.7 = (f32[32,64]{1,0:T(8,128)S(1)}, f32[32,64]{1,0:T(8,128)S(1)}, u32[]{:S(2)}, u32[]{:S(2)}) collective-permute-start(f32[32,64]{1,0:T(8,128)S(1)} %shard_map.68), channel_id=1, source_target_pairs={{0,4},{4,0},{8,12},{12,8},{16,20},{20,16},{24,28},{28,24},{1,5},{5... | collective-permute-start | bytes 24584 | tf_op jit(solution)/shard_map/ppermute | solution.py:301
  46.1 3.7 %collective-permute-start.8 = (f32[32,64]{1,0:T(8,128)S(1)}, f32[32,64]{1,0:T(8,128)S(1)}, u32[]{:S(2)}, u32[]{:S(2)}) collective-permute-start(f32[32,64]{1,0:T(8,128)S(1)} %add.21), channel_id=1, source_target_pairs={{0,8},{4,12},{8,0},{12,4},{16,24},{20,28},{24,16},{28,20},{1,9},{5... | collective-permute-start | bytes 24584 | tf_op jit(solution)/shard_map/ppermute | solution.py:301
  49.8 4.6 %collective-permute-start.9 = (f32[32,64]{1,0:T(8,128)S(1)}, f32[32,64]{1,0:T(8,128)S(1)}, u32[]{:S(2)}, u32[]{:S(2)}) collective-permute-start(f32[32,64]{1,0:T(8,128)S(1)} %add.22), channel_id=1, source_target_pairs={{0,16},{4,20},{8,24},{12,28},{16,0},{20,4},{24,8},{28,12},{1,17},{... | collective-permute-start | bytes 24584 | tf_op jit(solution)/shard_map/ppermute | solution.py:301

commit v2 on v1

--- a/solution.py
+++ b/solution.py
@@ -37,7 +37,7 @@
 ):
     mine, theirs = refs[:hops], refs[hops : 2 * hops]
     field_out, all_out, left_out = refs[2 * hops : 2 * hops + 3]
-    ext, low, high, scale, w0, d0, w1, d1, w2, b0, va, vb, b1, xa, xb, b2, ya, yb, kept = refs[2 * hops + 3 :]
+    ext, low, high, scale, w0, d0, w1, d1, w2, b0, va, vb, b1, xa, xb, b2, ya, yb, kept, ring = refs[2 * hops + 3 :]
     base = meta[0] * n - REACH
     even_group = meta[1] == 0
     own_slot = meta[2]
@@ -90,31 +90,56 @@
         for r in range(R):
             ref[layer * R + r, pl.ds(t * SUB, SUB), :] = values[r]
 
-    def around(below, here, above, weight):
+    cases = tiles * SUB
+    to = lax.broadcasted_iota(jnp.int32, (lanes, lanes), 0)
+    fro = lax.broadcasted_iota(jnp.int32, (lanes, lanes), 1)
+    step_apart = ((to - fro) % lanes == 1) | ((fro - to) % lanes == 1)
+    ring[...] = jnp.where(step_apart, 1.0, 0.0).astype(bf16)
+
+    def beside(x):
+        flat = x.reshape(-1, lanes)
+        top = flat.astype(bf16)
+        rest = (flat - top.astype(f32)).astype(bf16)
+        both = jnp.concatenate([top, rest], axis=1)
+        two = jnp.concatenate([ring[...], ring[...]], axis=0)
+        return jnp.dot(both, two, preferred_element_type=f32).reshape(x.shape)
+
+    def block(ref, layer, count):
+        return ref[pl.ds(layer * R, count * R)]
+
+    def neighbours(src, layer, count, weight):
+        by_matrix = [(i, r) for i in range(count) for r in range(R) if r % 2 == 0]
+        flat = [src[(layer + i) * R + r] for i, r in by_matrix]
+        got = beside(jnp.concatenate(flat, axis=0))
+        side = {key: got[j * cases : (j + 1) * cases] for j, key in enumerate(by_matrix)}
         out = []
-        for r in range(R):
-            axial = below[r] + above[r]
-            if weight != 1.0:
-                axial = weight * axial
-            side = pltpu.roll(here[r], 1, 1) + pltpu.roll(here[r], lanes - 1, 1)
-            if r > 0:
-                side = side + here[r - 1]
-            if r < R - 1:
-                side = side + here[r + 1]
-            out.append(axial + side)
+        for i in range(count):
+            line = []
+            for r in range(R):
+                axial = src[(layer + i - 1) * R + r] + src[(layer + i + 1) * R + r]
+                if weight != 1.0:
+                    axial = weight * axial
+                if (i, r) in side:
+                    beside_it = side[i, r]
+                else:
+                    here = src[(layer + i) * R + r]
+                    beside_it = jnp.concatenate([pltpu.roll(here[q * SUB : (q + 1) * SUB], 1, 1) + pltpu.roll(here[q * SUB : (q + 1) * SUB], lanes - 1, 1) for q in range(tiles)], axis=0)
+                x = axial + beside_it
+                if r > 0:
+                    x = x + src[(layer + i) * R + r - 1]
+                if r < R - 1:
+                    x = x + src[(layer + i) * R + r + 1]
+                line.append(x)
+            out.append(line)
         return out
 
     def sweep(src, dst, b, w, lo, hi, weight, fine, step=8):
         def body(layer, count):
-            for t in range(tiles):
-                v = [rows(src, layer + i - 1, t) for i in range(count + 2)]
-                new = []
-                for i in range(count):
-                    nv = around(v[i], v[i + 1], v[i + 2], weight)
-                    bb = rows(b, layer + i, t)
-                    new.append([(1.0 - damping) * v[i + 1][r] + node(w, layer + i, r, fine) * (bb[r] + nv[r]) for r in range(R)])
-                for i in range(count):
-                    put(dst, layer + i, t, new[i])
+            nv = neighbours(src, layer, count, weight)
+            for i in range(count):
+                for r in range(R):
+                    row = (layer + i) * R + r
+                    dst[row] = (1.0 - damping) * src[row] + node(w, layer + i, r, fine) * (b[row] + nv[i][r])
 
         over(lo, hi, step, body)
 
@@ -134,30 +159,28 @@
                     b0[(layer + i) * R + r, pl.ds(t * SUB, SUB), :] = value
                     va[(layer + i) * R + r, pl.ds(t * SUB, SUB), :] = value * w
 
-    def residual(src, b, d, layer, t, weight, fine):
-        v = [rows(src, layer + i - 1, t) for i in range(3)]
-        nv = around(v[0], v[1], v[2], weight)
-        bb = rows(b, layer, t)
-        return [bb[r] - node(d, layer, r, fine) * v[1][r] + nv[r] for r in range(R)]
+    def residual(src, b, d, layer, count, weight, fine):
+        nv = neighbours(src, layer, count, weight)
+        return [[b[(layer + i) * R + r] - node(d, layer + i, r, fine) * src[(layer + i) * R + r] + nv[i][r]
+                 for r in range(R)] for i in range(count)]
 
     def restrict(src, b, d, weight, fine, coarse_b, coarse_v, w, lo, hi, start, step):
-        for t in range(tiles):
-            put(kept, 0, t, residual(src, b, d, 2 * lo - 1, t, weight, fine))
+        first = residual(src, b, d, 2 * lo - 1, 1, weight, fine)[0]
+        for r in range(R):
+            kept[r] = first[r]
 
         def body(layer, count):
-            for t in range(tiles):
-                before = rows(kept, 0, t)
-                got = []
-                for i in range(count):
-                    even = residual(src, b, d, 2 * (layer + i), t, weight, fine)
-                    odd = residual(src, b, d, 2 * (layer + i) + 1, t, weight, fine)
-                    lead = jnp.where(layer + i + start > 0, 0.25, 0.0).astype(f32)
-                    got.append([0.5 * even[r] + (0.25 * odd[r] + lead * before[r]) for r in range(R)])
-                    before = odd
-                put(kept, 0, t, before)
-                for i in range(count):
-                    put(coarse_b, layer + i, t, got[i])
-                    put(coarse_v, layer + i, t, [got[i][r] * node(w, layer + i, r, False) for r in range(R)])
+            f = residual(src, b, d, 2 * layer, 2 * count, weight, fine)
+            for i in range(count):
+                lead = jnp.where(layer + i + start > 0, 0.25, 0.0).astype(f32)
+                for r in range(R):
+                    before = kept[r] if i == 0 else f[2 * i - 1][r]
+                    value = 0.5 * f[2 * i][r] + (0.25 * f[2 * i + 1][r] + lead * before)
+                    row = (layer + i) * R + r
+                    coarse_b[row] = value
+                    coarse_v[row] = value * node(w, layer + i, r, False)
+            for r in range(R):
+                kept[r] = f[-1][r]
 
         over(lo, hi, step, body)
 
@@ -175,43 +198,42 @@
         over(lo, hi, step, body)
 
     first, last = REACH - BELOW, REACH + n - 1 + ABOVE
-    over(first, last, 4, loads)
-    sweep(va, vb, b0, w0, first + 1, last - 1, 1.0, True)
+    over(first, last, 18, loads)
+    sweep(va, vb, b0, w0, first + 1, last - 1, 1.0, True, 23)
     mid, half = REACH // 2, n // 2
-    restrict(vb, b0, d0, 1.0, True, b1, xa, w1, mid - 13, mid + half + 13, base // 2, 5)
-    sweep(xa, xb, b1, w1, mid - 12, mid + half + 12, 0.25, False)
+    restrict(vb, b0, d0, 1.0, True, b1, xa, w1, mid - 13, mid + half + 13, base // 2, 11)
+    sweep(xa, xb, b1, w1, mid - 12, mid + half + 12, 0.25, False, 16)
     low_mid, quarter = REACH // 4, n // 4
-    restrict(xb, b1, d1, 0.25, False, b2, ya, w2, low_mid - 5, low_mid + quarter + 5, base // 4, 4)
-    sweep(ya, yb, b2, w2, low_mid - 4, low_mid + quarter + 4, 0.0625, False)
-    sweep(yb, ya, b2, w2, low_mid - 3, low_mid + quarter + 3, 0.0625, False)
-    sweep(ya, yb, b2, w2, low_mid - 2, low_mid + quarter + 2, 0.0625, False)
-    prolong(yb, xb, low_mid - 2, low_mid + quarter + 1, base // 4)
-    sweep(xb, xa, b1, w1, mid - 3, mid + half + 2, 0.25, False)
-    sweep(xa, xb, b1, w1, mid - 2, mid + half + 1, 0.25, False)
-    prolong(xb, vb, mid - 2, mid + half + 1, base // 2)
-    sweep(vb, va, b0, w0, REACH - 2, REACH + n + 1, 1.0, True)
-    sweep(va, vb, b0, w0, REACH - 1, REACH + n, 1.0, True)
+    restrict(xb, b1, d1, 0.25, False, b2, ya, w2, low_mid - 5, low_mid + quarter + 5, base // 4, 7)
+    sweep(ya, yb, b2, w2, low_mid - 4, low_mid + quarter + 4, 0.0625, False, 6)
+    sweep(yb, ya, b2, w2, low_mid - 3, low_mid + quarter + 3, 0.0625, False, 6)
+    sweep(ya, yb, b2, w2, low_mid - 2, low_mid + quarter + 2, 0.0625, False, 6)
+    prolong(yb, xb, low_mid - 2, low_mid + quarter + 1, base // 4, 7)
+    sweep(xb, xa, b1, w1, mid - 3, mid + half + 2, 0.25, False, 12)
+    sweep(xa, xb, b1, w1, mid - 2, mid + half + 1, 0.25, False, 12)
+    prolong(xb, vb, mid - 2, mid + half + 1, base // 2, 9)
+    sweep(vb, va, b0, w0, REACH - 2, REACH + n + 1, 1.0, True, 16)
+    sweep(va, vb, b0, w0, REACH - 1, REACH + n, 1.0, True, 16)
+
+    own = own_tiles * SUB
 
     def finish(layer, count):
+        nv = neighbours(vb, layer, count, 1.0)
         for i in range(count):
             for r in range(R):
-                all_out[(layer + i - REACH) * R + r] = vb[(layer + i) * R + r]
-        for t in range(own_tiles):
-            tile = own_slot * own_tiles + t
-
-            def at(ref, e, r):
-                return ref[e * R + r, pl.ds(pl.multiple_of(tile * SUB, SUB), SUB), :]
-
-            v = [[at(vb, layer + i - 1, r) for r in range(R)] for i in range(count + 2)]
-            for i in range(count):
-                nv = around(v[i], v[i + 1], v[i + 2], 1.0)
-                for r in range(R):
-                    row = (layer + i - REACH) * R + r
-                    field_out[pl.ds(t * SUB, SUB), row, :] = v[i + 1][r]
-                    left_out[row, pl.ds(t * SUB, SUB), :] = node(d0, layer + i, r, True) * v[i + 1][r] - nv[r]
-                    left_out[row, pl.ds((own_tiles + t) * SUB, SUB), :] = at(b0, layer + i, r)
-
-    over(REACH, REACH + n - 1, 4, finish)
+                at = (layer + i) * R + r
+                row = (layer + i - REACH) * R + r
+                here = vb[at]
+                all_out[row] = here
+                image = node(d0, layer + i, r, True) * here - nv[i][r]
+                load = b0[at]
+                def mine_of(x):
+                    return jnp.where(own_slot == 0, x[:own], x[own:])
+                field_out[:, row, :] = mine_of(here)
+                left_out[row, pl.ds(0, own), :] = mine_of(image)
+                left_out[row, pl.ds(own, own), :] = mine_of(load)
+
+    over(REACH, REACH + n - 1, 12, finish)
 
 
 def cycle(meta, table, panel, flags, diagonal, mine, theirs, cases, own, n, total, R):
@@ -235,6 +257,7 @@
         *(field(extent // 2) for _ in range(3)),
         *(field(extent // 4) for _ in range(3)),
         field(1),
+        pltpu.VMEM((lanes, lanes), bf16),
     ]
     vmem = pl.BlockSpec(memory_space=pltpu.VMEM)
     return pl.pallas_call(
@@ -251,45 +274,65 @@
     )(meta, table, panel, flags, diagonal, *mine, *theirs)
 
 
-def gram_kernel(meta, left, here, there, out, *, own):
-    even_group = meta[1] == 0
-    rows, cases, lanes = here.shape
-    slots = cases // own
-
-    def halves(x):
-        top = x.astype(bf16)
-        return top, (x - top.astype(f32)).astype(bf16)
-
-    def dot(a, b):
-        return lax.dot_general(a, b, (((1,), (1,)), ((), ())), preferred_element_type=f32)
-
-    together = 4
-
-    def trip(i, total):
-        a = jnp.concatenate([left[i * together + j] for j in range(together)], axis=1)
-        h = jnp.concatenate([here[i * together + j] for j in range(together)], axis=1)
-        o = jnp.concatenate([there[i * together + j] for j in range(together)], axis=1)
-        even, odd = jnp.where(even_group, h, o), jnp.where(even_group, o, h)
-        parts = []
-        for q in range(slots):
-            parts += [even[q * own : (q + 1) * own], odd[q * own : (q + 1) * own]]
-        b = jnp.concatenate(parts, axis=0)
+def halves(x):
+    top = x.astype(bf16)
+    return top, (x - top.astype(f32)).astype(bf16)
+
+
+def partial_products(left, right, together=12):
+    rows = right.shape[0]
+    total = 0.0
+    for i in range(0, rows, together):
+        a = jnp.concatenate([left[i + j] for j in range(together)], axis=1)
+        b = jnp.concatenate([right[i + j] for j in range(together)], axis=1)
         a_top, a_rest = halves(a)
         b_top, b_rest = halves(b)
-        return total + (dot(a_top, b_top) + (dot(a_top, b_rest) + dot(a_rest, b_top)))
-
-    out[...] = lax.fori_loop(0, rows // together, trip, jnp.zeros(out.shape, f32))
-
-
-def products(meta, left, here, there, own):
+
+        def dot(x, y):
+            return lax.dot_general(x, y, (((1,), (1,)), ((), ())), preferred_element_type=f32)
+
+        both = dot(jnp.concatenate([a_top, a_rest], axis=0), b_top)
+        total = total + (both[: a.shape[0]] + (both[a.shape[0] :] + dot(a_top, b_rest)))
+    return total
+
+
+def near_kernel(left, here, out):
+    out[...] = partial_products(left, here)
+
+
+def far_kernel(meta, left, there, near, out, *, own):
+    here, other = near[...], partial_products(left, there)
+    even_group = meta[1] == 0
+    even, odd = jnp.where(even_group, here, other), jnp.where(even_group, other, here)
+    parts = []
+    for q in range(here.shape[1] // own):
+        parts += [even[:, q * own : (q + 1) * own], odd[:, q * own : (q + 1) * own]]
+    out[...] = jnp.concatenate(parts, axis=1)
+
+
+def near_products(left, here):
+    rows, m, lanes = left.shape
+    cases = here.shape[1]
     vmem = pl.BlockSpec(memory_space=pltpu.VMEM)
     return pl.pallas_call(
-        functools.partial(gram_kernel, own=own),
-        out_shape=jax.ShapeDtypeStruct((left.shape[1], 2 * here.shape[1]), f32),
+        near_kernel,
+        out_shape=jax.ShapeDtypeStruct((m, cases), f32),
+        in_specs=[vmem] * 2,
+        out_specs=vmem,
+        cost_estimate=pl.CostEstimate(flops=6 * rows * m * cases * lanes, bytes_accessed=4 * rows * (m + cases) * lanes, transcendentals=0),
+        compiler_params=pltpu.CompilerParams(vmem_limit_bytes=32 * 2**20),
+    )(left, here)
+
+
+def far_products(meta, left, there, near, own):
+    vmem = pl.BlockSpec(memory_space=pltpu.VMEM)
+    return pl.pallas_call(
+        functools.partial(far_kernel, own=own),
+        out_shape=jax.ShapeDtypeStruct((near.shape[0], 2 * near.shape[1]), f32),
         in_specs=[pl.BlockSpec(memory_space=pltpu.SMEM)] + [vmem] * 3,
         out_specs=vmem,
         compiler_params=pltpu.CompilerParams(vmem_limit_bytes=32 * 2**20),
-    )(meta, left, here, there)
+    )(meta, left, there, near)
 
 
 def sum_over_slabs(x):
@@ -322,8 +365,8 @@
         pairs = []
         for s in range(slabs):
             for g in range(groups):
-                source = (s - k if g % 2 == 0 else s + k) % slabs
-                pairs.append((source * groups + g, s * groups + g))
+                to = s + k if g % 2 == 0 else s - k
+                pairs.append((s * groups + g, to * groups + g if 0 <= to < slabs else s * groups + (g ^ 1)))
         mine.append(lax.ppermute(block, ("slab", "case"), pairs))
     swap = [(g, g ^ 1) for g in range(groups)]
     theirs = [lax.ppermute(x, "case", swap) for x in mine]
@@ -334,7 +377,8 @@
 
     fields, worked, left = cycle(meta, table, *packed, mine, theirs, cases, own, n, total, R)
     received = lax.ppermute(worked, "case", swap)
-    sums = sum_over_slabs(products(meta, left, worked, received, own))
+    near = near_products(left, worked)
+    sums = sum_over_slabs(far_products(meta, left, received, near, own))
     sums = sums * (1.0 / (total * R * lanes))
     return fields.reshape(own, n, R, lanes), sums[:own], sums[own:]
 

time: 55.3 us -> 47.7 us (0.86)
  waiting for transfers between devices: 19.5 us -> 10.2 us
  starting transfers between devices: 8.72 us -> 15.4 us
  Pallas kernels: 23.9 us -> 18.9 us
    ppermute x3, starting transfers between devices: 1.48 us -> 7.64 us  [sum_over_slabs(): x = x + lax.ppermute(x, 'slab', [(i, i ^ by) for i in range(count)])]
    ppermute x3, waiting for transfers between devices: 10.7 us -> 5.97 us  [sum_over_slabs(): x = x + lax.ppermute(x, 'slab', [(i, i ^ by) for i in range(count)])]
    ppermute x3, waiting for transfers between devices: 5.51 us -> 1.38 us  [local(): mine.append(lax.ppermute(block, ('slab', 'case'), pairs))]
    pallas_call x1, Pallas kernels: 21.1 us -> 17.3 us  [cycle(): pl.pallas_call(functools.partial(cycle_kernel, tiles=cases // SUB, own_ti...]
    pallas_call x1 -> x2, Pallas kernels: 2.82 us -> 1.54 us  [the longest x1 1.08 us: far_products(): pl.pallas_call(functools.partial(far_kernel, own=own), out_shape=jax.Shap...]
    ppermute x3, starting transfers between devices: 0.01 us -> 0.56 us  [local(): theirs = [lax.ppermute(x, 'case', swap) for x in mine]]
  transfers between devices with their start and end apart: 10 -> 10, of which waited for: 8 -> 6; matrix products, arithmetic and copies ran while one was open for 0% -> 0% of each run, Pallas kernels for 0% -> 1%
where the time goes in v2:
time: 47.7 us; the launch traced here: 47.5 us
  Pallas kernels  18.9 us (40%)
  starting transfers between devices  15.4 us (32%)
  waiting for transfers between devices  10.2 us (21%)
  local copies, waits for them, and re-layouts  1.35 us (3%)
  other arithmetic  0.89 us (2%)
  between operations  0.71 us (1%)
    pallas_call x1, Pallas kernels, cycle(): pl.pallas_call(functools.partial(cycle_kernel, tiles=cases // SUB, own_ti...  17.3 us
    ppermute x3, starting transfers between devices, sum_over_slabs(): x = x + lax.ppermute(x, 'slab', [(i, i ^ by) for i in range(count)])  7.64 us
    ppermute x3, starting transfers between devices, local(): mine.append(lax.ppermute(block, ('slab', 'case'), pairs))  7.08 us
    ppermute x3, waiting for transfers between devices, sum_over_slabs(): x = x + lax.ppermute(x, 'slab', [(i, i ^ by) for i in range(count)])  5.97 us
    ppermute x1, waiting for transfers between devices, local(): received = lax.ppermute(worked, 'case', swap)  1.68 us
    ppermute x3, waiting for transfers between devices, local(): mine.append(lax.ppermute(block, ('slab', 'case'), pairs))  1.38 us
    ppermute x3, waiting for transfers between devices, local(): theirs = [lax.ppermute(x, 'case', swap) for x in mine]  1.19 us
    pallas_call x1, Pallas kernels, far_products(): pl.pallas_call(functools.partial(far_kernel, own=own), out_shape=jax.Shap...  1.08 us
  transfers between devices with their start and end apart: 10, of which 6 were waited for; matrix products, arithmetic and copies ran while one was open for 0% of the time, Pallas kernels for 1%

profile of v2, /device:TPU:0, one launch (start us, length us, event | category | flops | bytes accessed | tf_op | source)
XLA Modules:
  0.0 47.5 jit_solution(12639192075930880056)
XLA Ops:
  0.6 0.0 copy-start
  0.6 0.0 copy-start.2
  0.7 0.8 %convert_element_type.28 = f32[12,4,128]{2,1,0:T(4,128)S(1)} convert(s32[12,4,128]{2,1,0:T(4,128)} %param.6) | non-fusion elementwise | flops 6144 | bytes 49152 | tf_op jit(solution)/shard_map/convert_element_type | solution.py:361
  1.4 0.0 copy-done.2
  1.4 0.0 copy-start.1
  1.5 0.7 %copy-done.1 = f32[12,4,128]{2,1,0:T(4,128)S(1)} copy-done((f32[12,4,128]{2,1,0:T(4,128)S(1)}, f32[12,4,128]{2,1,0:T(4,128)}, u32[]{:S(2)}) %copy-start.1) | copy-done | bytes 24600
  2.2 3.0 %collective-permute-start = (f32[3,6,8,128]{3,2,1,0:T(8,128)S(1)}, f32[3,6,8,128]{3,2,1,0:T(8,128)S(1)}, u32[]{:S(2)}, u32[]{:S(2)}) collective-permute-start(f32[3,6,8,128]{3,2,1,0:T(8,128)S(1)} %pad_maximum_fusion), channel_id=1, source_target_pairs={{0,4},{1,0},{2,6},{3,2},{4,8},{5,1},{6,10},{7,3},{8,12},{9,5},{10,... | collective-permute-start | bytes 221192 | tf_op jit(solution)/shard_map/ppermute | solution.py:370
  5.2 1.6 %collective-permute-start.1 = (f32[3,6,8,128]{3,2,1,0:T(8,128)S(1)}, f32[3,6,8,128]{3,2,1,0:T(8,128)S(1)}, u32[]{:S(2)}, u32[]{:S(2)}) collective-permute-start(f32[3,6,8,128]{3,2,1,0:T(8,128)S(1)} %pad_maximum_fusion), channel_id=1, source_target_pairs={{0,8},{1,0},{2,10},{3,2},{4,12},{5,4},{6,14},{7,6},{8,16},{9,1},{1... | collective-permute-start | bytes 221192 | tf_op jit(solution)/shard_map/ppermute | solution.py:370
  6.7 2.5 %collective-permute-start.2 = (f32[3,6,8,128]{3,2,1,0:T(8,128)S(1)}, f32[3,6,8,128]{3,2,1,0:T(8,128)S(1)}, u32[]{:S(2)}, u32[]{:S(2)}) collective-permute-start(f32[3,6,8,128]{3,2,1,0:T(8,128)S(1)} %pad_maximum_fusion), channel_id=1, source_target_pairs={{0,12},{1,0},{2,14},{3,2},{4,16},{5,4},{6,18},{7,6},{8,20},{9,8},{... | collective-permute-start | bytes 221192 | tf_op jit(solution)/shard_map/ppermute | solution.py:370
  9.3 0.0 copy-done
  9.3 0.0 copy-start.3
  9.3 0.0 collective-permute-done.refs_0_
  9.3 0.1 collective-permute-start.3
  9.4 0.0 collective-permute-done.1.refs_1_
  9.4 0.5 %collective-permute-start.4 = (f32[3,6,8,128]{3,2,1,0:T(8,128)S(1)}, f32[3,6,8,128]{3,2,1,0:T(8,128)S(1)}, u32[]{:S(2)}, u32[]{:S(2)}) collective-permute-start(f32[3,6,8,128]{3,2,1,0:T(8,128)S(1)} %collective-permute-done.1.refs_1_), channel_id=1, source_target_pairs={{0,1},{1,0},{2,3},{3,2},{4,5},{5,4},{6,7},{7,6},{8,9},{9,8},{10,11... | collective-permute-start | bytes 221192 | tf_op jit(solution)/shard_map/ppermute | solution.py:372
  9.9 1.4 %collective-permute-done.2.refs_2_ = f32[3,6,8,128]{3,2,1,0:T(8,128)S(1)} collective-permute-done((f32[3,6,8,128]{3,2,1,0:T(8,128)S(1)}, f32[3,6,8,128]{3,2,1,0:T(8,128)S(1)}, u32[]{:S(2)}, u32[]{:S(2)}) %collective-permute-start.2) | collective-permute-done | bytes 73760 | tf_op jit(solution)/shard_map/ppermute | solution.py:370
  11.2 0.0 collective-permute-start.5
  11.3 0.1 pad_add_fusion.meta
  11.3 0.0 collective-permute-done.3.refs_3_
  11.3 0.0 collective-permute-done.4.refs_4_
  11.3 1.2 %collective-permute-done.5.refs_5_ = f32[3,6,8,128]{3,2,1,0:T(8,128)S(1)} collective-permute-done((f32[3,6,8,128]{3,2,1,0:T(8,128)S(1)}, f32[3,6,8,128]{3,2,1,0:T(8,128)S(1)}, u32[]{:S(2)}, u32[]{:S(2)}) %collective-permute-start.5) | collective-permute-done | bytes 73760 | tf_op jit(solution)/shard_map/ppermute | solution.py:372
  12.5 0.0 copy-done.3
  12.5 17.3 %shard_map.67 = (f32[16,48,128]{2,1,0:T(8,128)}, f32[48,32,128]{2,1,0:T(8,128)S(1)}, f32[48,32,128]{2,1,0:T(8,128)S(1)}) custom-call(s32[3]{0:T(128)S(1)} %pad_add_fusion.meta, f32[16,8,128]{2,1,0:T(8,128)S(1)} %bitcast.17, s32[6,8,128]{2,1,0:T(8,128)S(1)} %bitcast.20, s32[6,8,128]{2,1,0:T(8,128)S(1)} %bitcast.21, f32[6,8,128]{2,1,0:T(8,128)S(1)} %bitcast.19, ...), custom_call_target="tpu_custom_call" | custom-call | tf_op jit(solution)/shard_map/pallas_call | solution.py:263
  29.9 0.2 collective-permute-start.6
  30.0 0.5 shard_map.68.near
  30.5 1.7 %collective-permute-done.6.there = f32[48,32,128]{2,1,0:T(8,128)S(1)} collective-permute-done((f32[48,32,128]{2,1,0:T(8,128)S(1)}, f32[48,32,128]{2,1,0:T(8,128)S(1)}, u32[]{:S(2)}, u32[]{:S(2)}) %collective-permute-start.6) | collective-permute-done | bytes 786464 | tf_op jit(solution)/shard_map/ppermute | solution.py:379
  32.2 1.1 %shard_map.69 = f32[32,64]{1,0:T(8,128)S(1)} custom-call(s32[3]{0:T(128)S(1)} %pad_add_fusion.meta, f32[48,32,128]{2,1,0:T(8,128)S(1)} %get-tuple-element.7.left, f32[48,32,128]{2,1,0:T(8,128)S(1)} %collective-permute-done.6.there, f32[32,32]{1,0:T(8,128)S(1)} %shard_map.68.near), custom_call_target="tpu_custom_call" | custom-call | tf_op jit(solution)/shard_map/pallas_call | solution.py:329
  33.2 1.6 %collective-permute-start.7 = (f32[32,64]{1,0:T(8,128)S(1)}, f32[32,64]{1,0:T(8,128)S(1)}, u32[]{:S(2)}, u32[]{:S(2)}) collective-permute-start(f32[32,64]{1,0:T(8,128)S(1)} %shard_map.69), channel_id=1, source_target_pairs={{0,4},{4,0},{8,12},{12,8},{16,20},{20,16},{24,28},{28,24},{1,5},{5... | collective-permute-start | bytes 24584 | tf_op jit(solution)/shard_map/ppermute | solution.py:344
  34.8 2.2 %collective-permute-done.7 = f32[32,64]{1,0:T(8,128)S(1)} collective-permute-done((f32[32,64]{1,0:T(8,128)S(1)}, f32[32,64]{1,0:T(8,128)S(1)}, u32[]{:S(2)}, u32[]{:S(2)}) %collective-permute-start.7) | collective-permute-done | bytes 8224 | tf_op jit(solution)/shard_map/ppermute | solution.py:344
  37.1 1.8 %collective-permute-start.8 = (f32[32,64]{1,0:T(8,128)S(1)}, f32[32,64]{1,0:T(8,128)S(1)}, u32[]{:S(2)}, u32[]{:S(2)}) collective-permute-start(f32[32,64]{1,0:T(8,128)S(1)} %add.21), channel_id=1, source_target_pairs={{0,8},{4,12},{8,0},{12,4},{16,24},{20,28},{24,16},{28,20},{1,9},{5... | collective-permute-start | bytes 24584 | tf_op jit(solution)/shard_map/ppermute | solution.py:344
  38.9 1.9 %collective-permute-done.8 = f32[32,64]{1,0:T(8,128)S(1)} collective-permute-done((f32[32,64]{1,0:T(8,128)S(1)}, f32[32,64]{1,0:T(8,128)S(1)}, u32[]{:S(2)}, u32[]{:S(2)}) %collective-permute-start.8) | collective-permute-done | bytes 8224 | tf_op jit(solution)/shard_map/ppermute | solution.py:344
  40.8 4.2 %collective-permute-start.9 = (f32[32,64]{1,0:T(8,128)S(1)}, f32[32,64]{1,0:T(8,128)S(1)}, u32[]{:S(2)}, u32[]{:S(2)}) collective-permute-start(f32[32,64]{1,0:T(8,128)S(1)} %add.22), channel_id=1, source_target_pairs={{0,16},{4,20},{8,24},{12,28},{16,0},{20,4},{24,8},{28,12},{1,17},{... | collective-permute-start | bytes 24584 | tf_op jit(solution)/shard_map/ppermute | solution.py:344
  45.0 1.9 %collective-permute-done.9 = f32[32,64]{1,0:T(8,128)S(1)} collective-permute-done((f32[32,64]{1,0:T(8,128)S(1)}, f32[32,64]{1,0:T(8,128)S(1)}, u32[]{:S(2)}, u32[]{:S(2)}) %collective-permute-start.9) | collective-permute-done | bytes 8224 | tf_op jit(solution)/shard_map/ppermute | solution.py:344
  46.9 0.6 %fusion = (f32[16,64]{1,0:T(8,128)}, f32[16,64]{1,0:T(8,128)}) fusion(f32[32,64]{1,0:T(8,128)S(1)} %add_multiply_fusion), kind=kLoop, calls=%fused_computation.4 | loop fusion | bytes 16384 | tf_op jit(solution)/shard_map/slice | solution.py:383
  (6 shorter events, 0.0 us)
Async XLA Ops:
  0.6 8.6 %copy-start = (f32[64,512]{1,0:T(8,128)S(1)}, f32[64,512]{1,0:T(8,128)}, u32[]{:S(2)}) copy-start(f32[64,512]{1,0:T(8,128)} %param.4) | copy-start | bytes 393220
  0.6 0.8 %copy-start.2 = (s32[12,4,128]{2,1,0:T(4,128)S(1)}, s32[12,4,128]{2,1,0:T(4,128)}, u32[]{:S(2)}) copy-start(s32[12,4,128]{2,1,0:T(4,128)} %param.5) | copy-start | bytes 73732
  1.4 0.7 %copy-start.1 = (f32[12,4,128]{2,1,0:T(4,128)S(1)}, f32[12,4,128]{2,1,0:T(4,128)}, u32[]{:S(2)}) copy-start(f32[12,4,128]{2,1,0:T(4,128)} %param.7) | copy-start | bytes 73732
  2.2 7.1 %collective-permute-start = (f32[3,6,8,128]{3,2,1,0:T(8,128)S(1)}, f32[3,6,8,128]{3,2,1,0:T(8,128)S(1)}, u32[]{:S(2)}, u32[]{:S(2)}) collective-permute-start(f32[3,6,8,128]{3,2,1,0:T(8,128)S(1)} %pad_maximum_fusion), channel_id=1, source_target_pairs={{0,4},{1,0},{2,6},{3,2},{4,8},{5,1},{6,10},{7,3},{8,12},{9,5},{10,... | collective-permute-start | bytes 221192 | tf_op jit(solution)/shard_map/ppermute | solution.py:370
  5.2 4.2 %collective-permute-start.1 = (f32[3,6,8,128]{3,2,1,0:T(8,128)S(1)}, f32[3,6,8,128]{3,2,1,0:T(8,128)S(1)}, u32[]{:S(2)}, u32[]{:S(2)}) collective-permute-start(f32[3,6,8,128]{3,2,1,0:T(8,128)S(1)} %pad_maximum_fusion), channel_id=1, source_target_pairs={{0,8},{1,0},{2,10},{3,2},{4,12},{5,4},{6,14},{7,6},{8,16},{9,1},{1... | collective-permute-start | bytes 221192 | tf_op jit(solution)/shard_map/ppermute | solution.py:370
  6.7 4.5 %collective-permute-start.2 = (f32[3,6,8,128]{3,2,1,0:T(8,128)S(1)}, f32[3,6,8,128]{3,2,1,0:T(8,128)S(1)}, u32[]{:S(2)}, u32[]{:S(2)}) collective-permute-start(f32[3,6,8,128]{3,2,1,0:T(8,128)S(1)} %pad_maximum_fusion), channel_id=1, source_target_pairs={{0,12},{1,0},{2,14},{3,2},{4,16},{5,4},{6,18},{7,6},{8,20},{9,8},{... | collective-permute-start | bytes 221192 | tf_op jit(solution)/shard_map/ppermute | solution.py:370
  9.3 3.2 %copy-start.3 = (s32[12,4,128]{2,1,0:T(4,128)S(1)}, s32[12,4,128]{2,1,0:T(4,128)}, u32[]{:S(2)}) copy-start(s32[12,4,128]{2,1,0:T(4,128)} %param.6) | copy-start | bytes 73732
  9.3 2.0 %collective-permute-start.3 = (f32[3,6,8,128]{3,2,1,0:T(8,128)S(1)}, f32[3,6,8,128]{3,2,1,0:T(8,128)S(1)}, u32[]{:S(2)}, u32[]{:S(2)}) collective-permute-start(f32[3,6,8,128]{3,2,1,0:T(8,128)S(1)} %collective-permute-done.refs_0_), channel_id=1, source_target_pairs={{0,1},{1,0},{2,3},{3,2},{4,5},{5,4},{6,7},{7,6},{8,9},{9,8},{10,11... | collective-permute-start | bytes 221192 | tf_op jit(solution)/shard_map/ppermute | solution.py:372
  9.4 2.0 %collective-permute-start.4 = (f32[3,6,8,128]{3,2,1,0:T(8,128)S(1)}, f32[3,6,8,128]{3,2,1,0:T(8,128)S(1)}, u32[]{:S(2)}, u32[]{:S(2)}) collective-permute-start(f32[3,6,8,128]{3,2,1,0:T(8,128)S(1)} %collective-permute-done.1.refs_1_), channel_id=1, source_target_pairs={{0,1},{1,0},{2,3},{3,2},{4,5},{5,4},{6,7},{7,6},{8,9},{9,8},{10,11... | collective-permute-start | bytes 221192 | tf_op jit(solution)/shard_map/ppermute | solution.py:372
  11.2 1.3 %collective-permute-start.5 = (f32[3,6,8,128]{3,2,1,0:T(8,128)S(1)}, f32[3,6,8,128]{3,2,1,0:T(8,128)S(1)}, u32[]{:S(2)}, u32[]{:S(2)}) collective-permute-start(f32[3,6,8,128]{3,2,1,0:T(8,128)S(1)} %collective-permute-done.2.refs_2_), channel_id=1, source_target_pairs={{0,1},{1,0},{2,3},{3,2},{4,5},{5,4},{6,7},{7,6},{8,9},{9,8},{10,11... | collective-permute-start | bytes 221192 | tf_op jit(solution)/shard_map/ppermute | solution.py:372
  29.9 2.3 %collective-permute-start.6 = (f32[48,32,128]{2,1,0:T(8,128)S(1)}, f32[48,32,128]{2,1,0:T(8,128)S(1)}, u32[]{:S(2)}, u32[]{:S(2)}) collective-permute-start(f32[48,32,128]{2,1,0:T(8,128)S(1)} %get-tuple-element.8.here), channel_id=1, source_target_pairs={{0,1},{1,0},{2,3},{3,2},{4,5},{5,4},{6,7},{7,6},{8,9},{9,8},{10,11... | collective-permute-start | bytes 2359304 | tf_op jit(solution)/shard_map/ppermute | solution.py:379
  33.2 3.8 %collective-permute-start.7 = (f32[32,64]{1,0:T(8,128)S(1)}, f32[32,64]{1,0:T(8,128)S(1)}, u32[]{:S(2)}, u32[]{:S(2)}) collective-permute-start(f32[32,64]{1,0:T(8,128)S(1)} %shard_map.69), channel_id=1, source_target_pairs={{0,4},{4,0},{8,12},{12,8},{16,20},{20,16},{24,28},{28,24},{1,5},{5... | collective-permute-start | bytes 24584 | tf_op jit(solution)/shard_map/ppermute | solution.py:344
  37.1 3.7 %collective-permute-start.8 = (f32[32,64]{1,0:T(8,128)S(1)}, f32[32,64]{1,0:T(8,128)S(1)}, u32[]{:S(2)}, u32[]{:S(2)}) collective-permute-start(f32[32,64]{1,0:T(8,128)S(1)} %add.21), channel_id=1, source_target_pairs={{0,8},{4,12},{8,0},{12,4},{16,24},{20,28},{24,16},{28,20},{1,9},{5... | collective-permute-start | bytes 24584 | tf_op jit(solution)/shard_map/ppermute | solution.py:344
  40.8 6.1 %collective-permute-start.9 = (f32[32,64]{1,0:T(8,128)S(1)}, f32[32,64]{1,0:T(8,128)S(1)}, u32[]{:S(2)}, u32[]{:S(2)}) collective-permute-start(f32[32,64]{1,0:T(8,128)S(1)} %add.22), channel_id=1, source_target_pairs={{0,16},{4,20},{8,24},{12,28},{16,0},{20,4},{24,8},{28,12},{1,17},{... | collective-permute-start | bytes 24584 | tf_op jit(solution)/shard_map/ppermute | solution.py:344

commit v3 on v2

--- a/solution.py
+++ b/solution.py
@@ -37,7 +37,7 @@
 ):
     mine, theirs = refs[:hops], refs[hops : 2 * hops]
     field_out, all_out, left_out = refs[2 * hops : 2 * hops + 3]
-    ext, low, high, scale, w0, d0, w1, d1, w2, b0, va, vb, b1, xa, xb, b2, ya, yb, kept, ring = refs[2 * hops + 3 :]
+    ext, picked, scale, w0, d0, w1, d1, w2, b0, va, vb, b1, xa, xb, b2, ya, yb, kept, ring, stack = refs[2 * hops + 3 :]
     base = meta[0] * n - REACH
     even_group = meta[1] == 0
     own_slot = meta[2]
@@ -65,8 +65,7 @@
     span = 1.0 + 2.0 * position.astype(f32) / total
     scale[...] = jnp.where(inside, span * (1.0 - held), 0.0).reshape(scale.shape)
     index = ext[0].astype(jnp.int32)
-    low[...] = (index % lanes).reshape(low.shape)
-    high[...] = (index // lanes).reshape(high.shape)
+    picked[...] = index.reshape(picked.shape)
     d = coeff + 6.0
     d0[...] = d.reshape(d0.shape)
     w0[...] = jnp.where(inside, damping / d, 0.0).reshape(w0.shape)
@@ -143,21 +142,45 @@
 
         over(lo, hi, step, body)
 
+    pair = 2 * lanes
+    wide = quads // 2
+    for h in range(wide):
+        both = jnp.concatenate([jnp.concatenate([table[t * quads + 2 * h], table[t * quads + 2 * h + 1]], axis=1) for t in range(tiles)], axis=0)
+        top = both.astype(bf16)
+        stack[pl.ds(2 * h * cases, cases), :] = top
+        stack[pl.ds((2 * h + 1) * cases, cases), :] = (both - top.astype(f32)).astype(bf16)
+
+    def by_matrix(index):
+        spot = lax.broadcasted_iota(jnp.int16, (pair, lanes), 0)
+        place = jnp.broadcast_to(index & (pair - 1), (2 * SUB, lanes)).astype(jnp.int16)
+        place = jnp.concatenate([place] * (pair // (2 * SUB)), axis=0)
+        hot = jnp.where(spot == place, jnp.ones((), bf16), jnp.zeros((), bf16))
+        got = jnp.dot(stack[...], hot, preferred_element_type=f32)
+        value = got[:cases] + got[cases : 2 * cases]
+        for h in range(1, wide):
+            value = jnp.where(jnp.broadcast_to(index, value.shape) >= h * pair, got[2 * h * cases : (2 * h + 1) * cases] + got[(2 * h + 1) * cases : (2 * h + 2) * cases], value)
+        return value
+
+    def by_lanes(index):
+        wide_index = jnp.broadcast_to(index, (SUB, lanes))
+        low = jnp.broadcast_to(index & (lanes - 1), (SUB, lanes))
+        beyond = [wide_index >= q * lanes for q in range(1, quads)]
+        out = []
+        for t in range(tiles):
+            value = jnp.take_along_axis(table[t * quads], low, axis=1)
+            for q in range(1, quads):
+                value = jnp.where(beyond[q - 1], jnp.take_along_axis(table[t * quads + q], low, axis=1), value)
+            out.append(value)
+        return jnp.concatenate(out, axis=0)
+
     def loads(layer, count):
         for i in range(count):
             for r in range(R):
-                lo = jnp.broadcast_to(node(low, layer + i, r, True), (SUB, lanes))
-                hi = jnp.broadcast_to(node(high, layer + i, r, True), (SUB, lanes))
-                factor = node(scale, layer + i, r, True)
-                w = node(w0, layer + i, r, True)
-                at = [hi == q for q in range(quads)]
-                for t in range(tiles):
-                    value = jnp.take_along_axis(table[t * quads], lo, axis=1)
-                    for q in range(1, quads):
-                        value = jnp.where(at[q], jnp.take_along_axis(table[t * quads + q], lo, axis=1), value)
-                    value = value * factor
-                    b0[(layer + i) * R + r, pl.ds(t * SUB, SUB), :] = value
-                    va[(layer + i) * R + r, pl.ds(t * SUB, SUB), :] = value * w
+                index = node(picked, layer + i, r, True)
+                value = by_matrix(index) if r % 2 else by_lanes(index)
+                value = value * node(scale, layer + i, r, True)
+                b0[(layer + i) * R + r] = value
+                va[(layer + i) * R + r] = value * node(w0, layer + i, r, True)
 
     def residual(src, b, d, layer, count, weight, fine):
         nv = neighbours(src, layer, count, weight)
@@ -204,10 +227,10 @@
     restrict(vb, b0, d0, 1.0, True, b1, xa, w1, mid - 13, mid + half + 13, base // 2, 11)
     sweep(xa, xb, b1, w1, mid - 12, mid + half + 12, 0.25, False, 16)
     low_mid, quarter = REACH // 4, n // 4
-    restrict(xb, b1, d1, 0.25, False, b2, ya, w2, low_mid - 5, low_mid + quarter + 5, base // 4, 7)
-    sweep(ya, yb, b2, w2, low_mid - 4, low_mid + quarter + 4, 0.0625, False, 6)
-    sweep(yb, ya, b2, w2, low_mid - 3, low_mid + quarter + 3, 0.0625, False, 6)
-    sweep(ya, yb, b2, w2, low_mid - 2, low_mid + quarter + 2, 0.0625, False, 6)
+    restrict(xb, b1, d1, 0.25, False, b2, ya, w2, low_mid - 5, low_mid + quarter + 5, base // 4, 14)
+    sweep(ya, yb, b2, w2, low_mid - 4, low_mid + quarter + 4, 0.0625, False, 12)
+    sweep(yb, ya, b2, w2, low_mid - 3, low_mid + quarter + 3, 0.0625, False, 12)
+    sweep(ya, yb, b2, w2, low_mid - 2, low_mid + quarter + 2, 0.0625, False, 12)
     prolong(yb, xb, low_mid - 2, low_mid + quarter + 1, base // 4, 7)
     sweep(xb, xa, b1, w1, mid - 3, mid + half + 2, 0.25, False, 12)
     sweep(xa, xb, b1, w1, mid - 2, mid + half + 1, 0.25, False, 12)
@@ -251,13 +274,13 @@
     scratch = [
         pltpu.VMEM((3, fine // SUB, SUB, lanes), f32),
         coefficients(fine, jnp.int32),
-        coefficients(fine, jnp.int32),
         *(coefficients(rows) for rows in (fine, fine, fine, middle, middle, coarse)),
         *(field(extent) for _ in range(3)),
         *(field(extent // 2) for _ in range(3)),
         *(field(extent // 4) for _ in range(3)),
         field(1),
         pltpu.VMEM((lanes, lanes), bf16),
+        pltpu.VMEM((cases * table.shape[0] * SUB // cases, 2 * lanes), bf16),
     ]
     vmem = pl.BlockSpec(memory_space=pltpu.VMEM)
     return pl.pallas_call(

time: 47.7 us -> 44.5 us (0.933)
  Pallas kernels: 18.9 us -> 15.7 us
    pallas_call x1, Pallas kernels: 17.3 us -> 14.1 us  [cycle(): pl.pallas_call(functools.partial(cycle_kernel, tiles=cases // SUB, own_ti...]
where the time goes in v3:
time: 44.5 us; the launch traced here: 44.3 us
  Pallas kernels  15.7 us (35%)
  starting transfers between devices  15.4 us (35%)
  waiting for transfers between devices  10.2 us (23%)
  local copies, waits for them, and re-layouts  1.35 us (3%)
  other arithmetic  0.89 us (2%)
  between operations  0.71 us (2%)
    pallas_call x1, Pallas kernels, cycle(): pl.pallas_call(functools.partial(cycle_kernel, tiles=cases // SUB, own_ti...  14.1 us
    ppermute x3, starting transfers between devices, sum_over_slabs(): x = x + lax.ppermute(x, 'slab', [(i, i ^ by) for i in range(count)])  7.63 us
    ppermute x3, starting transfers between devices, local(): mine.append(lax.ppermute(block, ('slab', 'case'), pairs))  7.08 us
    ppermute x3, waiting for transfers between devices, sum_over_slabs(): x = x + lax.ppermute(x, 'slab', [(i, i ^ by) for i in range(count)])  5.98 us
    ppermute x1, waiting for transfers between devices, local(): received = lax.ppermute(worked, 'case', swap)  1.69 us
    ppermute x3, waiting for transfers between devices, local(): mine.append(lax.ppermute(block, ('slab', 'case'), pairs))  1.38 us
    ppermute x3, waiting for transfers between devices, local(): theirs = [lax.ppermute(x, 'case', swap) for x in mine]  1.19 us
    pallas_call x1, Pallas kernels, far_products(): pl.pallas_call(functools.partial(far_kernel, own=own), out_shape=jax.Shap...  1.08 us
  transfers between devices with their start and end apart: 10, of which 6 were waited for; matrix products, arithmetic and copies ran while one was open for 0% of the time, Pallas kernels for 1%

profile of v3, /device:TPU:0, one launch (start us, length us, event | category | flops | bytes accessed | tf_op | source)
XLA Modules:
  0.0 44.3 jit_solution(12142624828574556243)
XLA Ops:
  0.6 0.0 copy-start
  0.6 0.0 copy-start.2
  0.7 0.8 %convert_element_type.28 = f32[12,4,128]{2,1,0:T(4,128)S(1)} convert(s32[12,4,128]{2,1,0:T(4,128)} %param.6) | non-fusion elementwise | flops 6144 | bytes 49152 | tf_op jit(solution)/shard_map/convert_element_type | solution.py:384
  1.4 0.0 copy-done.2
  1.4 0.0 copy-start.1
  1.5 0.7 %copy-done.1 = f32[12,4,128]{2,1,0:T(4,128)S(1)} copy-done((f32[12,4,128]{2,1,0:T(4,128)S(1)}, f32[12,4,128]{2,1,0:T(4,128)}, u32[]{:S(2)}) %copy-start.1) | copy-done | bytes 24600
  2.2 3.0 %collective-permute-start = (f32[3,6,8,128]{3,2,1,0:T(8,128)S(1)}, f32[3,6,8,128]{3,2,1,0:T(8,128)S(1)}, u32[]{:S(2)}, u32[]{:S(2)}) collective-permute-start(f32[3,6,8,128]{3,2,1,0:T(8,128)S(1)} %pad_maximum_fusion), channel_id=1, source_target_pairs={{0,4},{1,0},{2,6},{3,2},{4,8},{5,1},{6,10},{7,3},{8,12},{9,5},{10,... | collective-permute-start | bytes 221192 | tf_op jit(solution)/shard_map/ppermute | solution.py:393
  5.2 1.6 %collective-permute-start.1 = (f32[3,6,8,128]{3,2,1,0:T(8,128)S(1)}, f32[3,6,8,128]{3,2,1,0:T(8,128)S(1)}, u32[]{:S(2)}, u32[]{:S(2)}) collective-permute-start(f32[3,6,8,128]{3,2,1,0:T(8,128)S(1)} %pad_maximum_fusion), channel_id=1, source_target_pairs={{0,8},{1,0},{2,10},{3,2},{4,12},{5,4},{6,14},{7,6},{8,16},{9,1},{1... | collective-permute-start | bytes 221192 | tf_op jit(solution)/shard_map/ppermute | solution.py:393
  6.7 2.5 %collective-permute-start.2 = (f32[3,6,8,128]{3,2,1,0:T(8,128)S(1)}, f32[3,6,8,128]{3,2,1,0:T(8,128)S(1)}, u32[]{:S(2)}, u32[]{:S(2)}) collective-permute-start(f32[3,6,8,128]{3,2,1,0:T(8,128)S(1)} %pad_maximum_fusion), channel_id=1, source_target_pairs={{0,12},{1,0},{2,14},{3,2},{4,16},{5,4},{6,18},{7,6},{8,20},{9,8},{... | collective-permute-start | bytes 221192 | tf_op jit(solution)/shard_map/ppermute | solution.py:393
  9.3 0.0 copy-done
  9.3 0.0 copy-start.3
  9.3 0.0 collective-permute-done.refs_0_
  9.3 0.1 collective-permute-start.3
  9.4 0.0 collective-permute-done.1.refs_1_
  9.4 0.5 %collective-permute-start.4 = (f32[3,6,8,128]{3,2,1,0:T(8,128)S(1)}, f32[3,6,8,128]{3,2,1,0:T(8,128)S(1)}, u32[]{:S(2)}, u32[]{:S(2)}) collective-permute-start(f32[3,6,8,128]{3,2,1,0:T(8,128)S(1)} %collective-permute-done.1.refs_1_), channel_id=1, source_target_pairs={{0,1},{1,0},{2,3},{3,2},{4,5},{5,4},{6,7},{7,6},{8,9},{9,8},{10,11... | collective-permute-start | bytes 221192 | tf_op jit(solution)/shard_map/ppermute | solution.py:395
  9.9 1.4 %collective-permute-done.2.refs_2_ = f32[3,6,8,128]{3,2,1,0:T(8,128)S(1)} collective-permute-done((f32[3,6,8,128]{3,2,1,0:T(8,128)S(1)}, f32[3,6,8,128]{3,2,1,0:T(8,128)S(1)}, u32[]{:S(2)}, u32[]{:S(2)}) %collective-permute-start.2) | collective-permute-done | bytes 73760 | tf_op jit(solution)/shard_map/ppermute | solution.py:393
  11.2 0.0 collective-permute-start.5
  11.3 0.1 pad_add_fusion.meta
  11.3 0.0 collective-permute-done.3.refs_3_
  11.3 0.0 collective-permute-done.4.refs_4_
  11.3 1.2 %collective-permute-done.5.refs_5_ = f32[3,6,8,128]{3,2,1,0:T(8,128)S(1)} collective-permute-done((f32[3,6,8,128]{3,2,1,0:T(8,128)S(1)}, f32[3,6,8,128]{3,2,1,0:T(8,128)S(1)}, u32[]{:S(2)}, u32[]{:S(2)}) %collective-permute-start.5) | collective-permute-done | bytes 73760 | tf_op jit(solution)/shard_map/ppermute | solution.py:395
  12.5 0.0 copy-done.3
  12.5 14.1 %shard_map.67 = (f32[16,48,128]{2,1,0:T(8,128)}, f32[48,32,128]{2,1,0:T(8,128)S(1)}, f32[48,32,128]{2,1,0:T(8,128)S(1)}) custom-call(s32[3]{0:T(128)S(1)} %pad_add_fusion.meta, f32[16,8,128]{2,1,0:T(8,128)S(1)} %bitcast.17, s32[6,8,128]{2,1,0:T(8,128)S(1)} %bitcast.20, s32[6,8,128]{2,1,0:T(8,128)S(1)} %bitcast.21, f32[6,8,128]{2,1,0:T(8,128)S(1)} %bitcast.19, ...), custom_call_target="tpu_custom_call" | custom-call | tf_op jit(solution)/shard_map/pallas_call | solution.py:286
  26.7 0.2 collective-permute-start.6
  26.8 0.4 %shard_map.68.near = f32[32,32]{1,0:T(8,128)S(1)} custom-call(f32[48,32,128]{2,1,0:T(8,128)S(1)} %get-tuple-element.7.left, f32[48,32,128]{2,1,0:T(8,128)S(1)} %get-tuple-element.8.here), custom_call_target="tpu_custom_call" | custom-call | flops 37748736 | bytes 1572864 | tf_op jit(solution)/shard_map/pallas_call | solution.py:340
  27.3 1.7 %collective-permute-done.6.there = f32[48,32,128]{2,1,0:T(8,128)S(1)} collective-permute-done((f32[48,32,128]{2,1,0:T(8,128)S(1)}, f32[48,32,128]{2,1,0:T(8,128)S(1)}, u32[]{:S(2)}, u32[]{:S(2)}) %collective-permute-start.6) | collective-permute-done | bytes 786464 | tf_op jit(solution)/shard_map/ppermute | solution.py:402
  28.9 1.1 %shard_map.69 = f32[32,64]{1,0:T(8,128)S(1)} custom-call(s32[3]{0:T(128)S(1)} %pad_add_fusion.meta, f32[48,32,128]{2,1,0:T(8,128)S(1)} %get-tuple-element.7.left, f32[48,32,128]{2,1,0:T(8,128)S(1)} %collective-permute-done.6.there, f32[32,32]{1,0:T(8,128)S(1)} %shard_map.68.near), custom_call_target="tpu_custom_call" | custom-call | tf_op jit(solution)/shard_map/pallas_call | solution.py:352
  30.0 1.6 %collective-permute-start.7 = (f32[32,64]{1,0:T(8,128)S(1)}, f32[32,64]{1,0:T(8,128)S(1)}, u32[]{:S(2)}, u32[]{:S(2)}) collective-permute-start(f32[32,64]{1,0:T(8,128)S(1)} %shard_map.69), channel_id=1, source_target_pairs={{0,4},{4,0},{8,12},{12,8},{16,20},{20,16},{24,28},{28,24},{1,5},{5... | collective-permute-start | bytes 24584 | tf_op jit(solution)/shard_map/ppermute | solution.py:367
  31.6 2.2 %collective-permute-done.7 = f32[32,64]{1,0:T(8,128)S(1)} collective-permute-done((f32[32,64]{1,0:T(8,128)S(1)}, f32[32,64]{1,0:T(8,128)S(1)}, u32[]{:S(2)}, u32[]{:S(2)}) %collective-permute-start.7) | collective-permute-done | bytes 8224 | tf_op jit(solution)/shard_map/ppermute | solution.py:367
  33.9 1.8 %collective-permute-start.8 = (f32[32,64]{1,0:T(8,128)S(1)}, f32[32,64]{1,0:T(8,128)S(1)}, u32[]{:S(2)}, u32[]{:S(2)}) collective-permute-start(f32[32,64]{1,0:T(8,128)S(1)} %add.21), channel_id=1, source_target_pairs={{0,8},{4,12},{8,0},{12,4},{16,24},{20,28},{24,16},{28,20},{1,9},{5... | collective-permute-start | bytes 24584 | tf_op jit(solution)/shard_map/ppermute | solution.py:367
  35.7 1.9 %collective-permute-done.8 = f32[32,64]{1,0:T(8,128)S(1)} collective-permute-done((f32[32,64]{1,0:T(8,128)S(1)}, f32[32,64]{1,0:T(8,128)S(1)}, u32[]{:S(2)}, u32[]{:S(2)}) %collective-permute-start.8) | collective-permute-done | bytes 8224 | tf_op jit(solution)/shard_map/ppermute | solution.py:367
  37.6 4.2 %collective-permute-start.9 = (f32[32,64]{1,0:T(8,128)S(1)}, f32[32,64]{1,0:T(8,128)S(1)}, u32[]{:S(2)}, u32[]{:S(2)}) collective-permute-start(f32[32,64]{1,0:T(8,128)S(1)} %add.22), channel_id=1, source_target_pairs={{0,16},{4,20},{8,24},{12,28},{16,0},{20,4},{24,8},{28,12},{1,17},{... | collective-permute-start | bytes 24584 | tf_op jit(solution)/shard_map/ppermute | solution.py:367
  41.8 1.8 %collective-permute-done.9 = f32[32,64]{1,0:T(8,128)S(1)} collective-permute-done((f32[32,64]{1,0:T(8,128)S(1)}, f32[32,64]{1,0:T(8,128)S(1)}, u32[]{:S(2)}, u32[]{:S(2)}) %collective-permute-start.9) | collective-permute-done | bytes 8224 | tf_op jit(solution)/shard_map/ppermute | solution.py:367
  43.7 0.6 %fusion = (f32[16,64]{1,0:T(8,128)}, f32[16,64]{1,0:T(8,128)}) fusion(f32[32,64]{1,0:T(8,128)S(1)} %add_multiply_fusion), kind=kLoop, calls=%fused_computation.4 | loop fusion | bytes 16384 | tf_op jit(solution)/shard_map/slice | solution.py:406
  (6 shorter events, 0.0 us)
Async XLA Ops:
  0.6 8.6 %copy-start = (f32[64,512]{1,0:T(8,128)S(1)}, f32[64,512]{1,0:T(8,128)}, u32[]{:S(2)}) copy-start(f32[64,512]{1,0:T(8,128)} %param.4) | copy-start | bytes 393220
  0.6 0.8 %copy-start.2 = (s32[12,4,128]{2,1,0:T(4,128)S(1)}, s32[12,4,128]{2,1,0:T(4,128)}, u32[]{:S(2)}) copy-start(s32[12,4,128]{2,1,0:T(4,128)} %param.5) | copy-start | bytes 73732
  1.4 0.7 %copy-start.1 = (f32[12,4,128]{2,1,0:T(4,128)S(1)}, f32[12,4,128]{2,1,0:T(4,128)}, u32[]{:S(2)}) copy-start(f32[12,4,128]{2,1,0:T(4,128)} %param.7) | copy-start | bytes 73732
  2.2 7.1 %collective-permute-start = (f32[3,6,8,128]{3,2,1,0:T(8,128)S(1)}, f32[3,6,8,128]{3,2,1,0:T(8,128)S(1)}, u32[]{:S(2)}, u32[]{:S(2)}) collective-permute-start(f32[3,6,8,128]{3,2,1,0:T(8,128)S(1)} %pad_maximum_fusion), channel_id=1, source_target_pairs={{0,4},{1,0},{2,6},{3,2},{4,8},{5,1},{6,10},{7,3},{8,12},{9,5},{10,... | collective-permute-start | bytes 221192 | tf_op jit(solution)/shard_map/ppermute | solution.py:393
  5.2 4.2 %collective-permute-start.1 = (f32[3,6,8,128]{3,2,1,0:T(8,128)S(1)}, f32[3,6,8,128]{3,2,1,0:T(8,128)S(1)}, u32[]{:S(2)}, u32[]{:S(2)}) collective-permute-start(f32[3,6,8,128]{3,2,1,0:T(8,128)S(1)} %pad_maximum_fusion), channel_id=1, source_target_pairs={{0,8},{1,0},{2,10},{3,2},{4,12},{5,4},{6,14},{7,6},{8,16},{9,1},{1... | collective-permute-start | bytes 221192 | tf_op jit(solution)/shard_map/ppermute | solution.py:393
  6.7 4.5 %collective-permute-start.2 = (f32[3,6,8,128]{3,2,1,0:T(8,128)S(1)}, f32[3,6,8,128]{3,2,1,0:T(8,128)S(1)}, u32[]{:S(2)}, u32[]{:S(2)}) collective-permute-start(f32[3,6,8,128]{3,2,1,0:T(8,128)S(1)} %pad_maximum_fusion), channel_id=1, source_target_pairs={{0,12},{1,0},{2,14},{3,2},{4,16},{5,4},{6,18},{7,6},{8,20},{9,8},{... | collective-permute-start | bytes 221192 | tf_op jit(solution)/shard_map/ppermute | solution.py:393
  9.3 3.2 %copy-start.3 = (s32[12,4,128]{2,1,0:T(4,128)S(1)}, s32[12,4,128]{2,1,0:T(4,128)}, u32[]{:S(2)}) copy-start(s32[12,4,128]{2,1,0:T(4,128)} %param.6) | copy-start | bytes 73732
  9.3 2.0 %collective-permute-start.3 = (f32[3,6,8,128]{3,2,1,0:T(8,128)S(1)}, f32[3,6,8,128]{3,2,1,0:T(8,128)S(1)}, u32[]{:S(2)}, u32[]{:S(2)}) collective-permute-start(f32[3,6,8,128]{3,2,1,0:T(8,128)S(1)} %collective-permute-done.refs_0_), channel_id=1, source_target_pairs={{0,1},{1,0},{2,3},{3,2},{4,5},{5,4},{6,7},{7,6},{8,9},{9,8},{10,11... | collective-permute-start | bytes 221192 | tf_op jit(solution)/shard_map/ppermute | solution.py:395
  9.4 2.0 %collective-permute-start.4 = (f32[3,6,8,128]{3,2,1,0:T(8,128)S(1)}, f32[3,6,8,128]{3,2,1,0:T(8,128)S(1)}, u32[]{:S(2)}, u32[]{:S(2)}) collective-permute-start(f32[3,6,8,128]{3,2,1,0:T(8,128)S(1)} %collective-permute-done.1.refs_1_), channel_id=1, source_target_pairs={{0,1},{1,0},{2,3},{3,2},{4,5},{5,4},{6,7},{7,6},{8,9},{9,8},{10,11... | collective-permute-start | bytes 221192 | tf_op jit(solution)/shard_map/ppermute | solution.py:395
  11.2 1.3 %collective-permute-start.5 = (f32[3,6,8,128]{3,2,1,0:T(8,128)S(1)}, f32[3,6,8,128]{3,2,1,0:T(8,128)S(1)}, u32[]{:S(2)}, u32[]{:S(2)}) collective-permute-start(f32[3,6,8,128]{3,2,1,0:T(8,128)S(1)} %collective-permute-done.2.refs_2_), channel_id=1, source_target_pairs={{0,1},{1,0},{2,3},{3,2},{4,5},{5,4},{6,7},{7,6},{8,9},{9,8},{10,11... | collective-permute-start | bytes 221192 | tf_op jit(solution)/shard_map/ppermute | solution.py:395
  26.7 2.3 %collective-permute-start.6 = (f32[48,32,128]{2,1,0:T(8,128)S(1)}, f32[48,32,128]{2,1,0:T(8,128)S(1)}, u32[]{:S(2)}, u32[]{:S(2)}) collective-permute-start(f32[48,32,128]{2,1,0:T(8,128)S(1)} %get-tuple-element.8.here), channel_id=1, source_target_pairs={{0,1},{1,0},{2,3},{3,2},{4,5},{5,4},{6,7},{7,6},{8,9},{9,8},{10,11... | collective-permute-start | bytes 2359304 | tf_op jit(solution)/shard_map/ppermute | solution.py:402
  30.0 3.8 %collective-permute-start.7 = (f32[32,64]{1,0:T(8,128)S(1)}, f32[32,64]{1,0:T(8,128)S(1)}, u32[]{:S(2)}, u32[]{:S(2)}) collective-permute-start(f32[32,64]{1,0:T(8,128)S(1)} %shard_map.69), channel_id=1, source_target_pairs={{0,4},{4,0},{8,12},{12,8},{16,20},{20,16},{24,28},{28,24},{1,5},{5... | collective-permute-start | bytes 24584 | tf_op jit(solution)/shard_map/ppermute | solution.py:367
  33.9 3.7 %collective-permute-start.8 = (f32[32,64]{1,0:T(8,128)S(1)}, f32[32,64]{1,0:T(8,128)S(1)}, u32[]{:S(2)}, u32[]{:S(2)}) collective-permute-start(f32[32,64]{1,0:T(8,128)S(1)} %add.21), channel_id=1, source_target_pairs={{0,8},{4,12},{8,0},{12,4},{16,24},{20,28},{24,16},{28,20},{1,9},{5... | collective-permute-start | bytes 24584 | tf_op jit(solution)/shard_map/ppermute | solution.py:367
  37.6 6.1 %collective-permute-start.9 = (f32[32,64]{1,0:T(8,128)S(1)}, f32[32,64]{1,0:T(8,128)S(1)}, u32[]{:S(2)}, u32[]{:S(2)}) collective-permute-start(f32[32,64]{1,0:T(8,128)S(1)} %add.22), channel_id=1, source_target_pairs={{0,16},{4,20},{8,24},{12,28},{16,0},{20,4},{24,8},{28,12},{1,17},{... | collective-permute-start | bytes 24584 | tf_op jit(solution)/shard_map/ppermute | solution.py:367

commit v4 on v3

--- a/solution.py
+++ b/solution.py
@@ -33,21 +33,23 @@
 
 
 def cycle_kernel(
-    meta, table, panel, flags, diagonal, *refs, tiles, own_tiles, n, total, R, hops
+    table, block, *refs, tiles, own_tiles, n, total, R, hops
 ):
     mine, theirs = refs[:hops], refs[hops : 2 * hops]
-    field_out, all_out, left_out = refs[2 * hops : 2 * hops + 3]
-    ext, picked, scale, w0, d0, w1, d1, w2, b0, va, vb, b1, xa, xb, b2, ya, yb, kept, ring, stack = refs[2 * hops + 3 :]
-    base = meta[0] * n - REACH
-    even_group = meta[1] == 0
-    own_slot = meta[2]
+    field_out, first_out, second_out, left_out = refs[2 * hops : 2 * hops + 4]
+    split = first_out.shape[0]
+    ext, picked, scale, w0, d0, w1, d1, w2, b0, va, vb, b1, xa, xb, b2, ya, yb, kept, ring, stack = refs[2 * hops + 4 :]
+    base = lax.axis_index("slab") * n - REACH
+    group = lax.axis_index("case")
+    even_group = group % 2 == 0
+    own_slot = group // 2
     lanes = table.shape[-1]
     quads = table.shape[0] // tiles
     per = SUB // R
 
     near = n // per
-    for which, own in enumerate((panel, flags, diagonal)):
-        ext[which, pl.ds(REACH // per, near)] = own[...].astype(f32)
+    for which in range(3):
+        ext[which, pl.ds(REACH // per, near)] = block[which]
     for k in range(1, hops + 1):
         depth = min(n, REACH - (k - 1) * n) // per
         below = (REACH - (k - 1) * n) // per - depth
@@ -247,7 +249,10 @@
                 at = (layer + i) * R + r
                 row = (layer + i - REACH) * R + r
                 here = vb[at]
-                all_out[row] = here
+                if row < split:
+                    first_out[row] = here
+                else:
+                    second_out[row - split] = here
                 image = node(d0, layer + i, r, True) * here - nv[i][r]
                 load = b0[at]
                 def mine_of(x):
@@ -259,7 +264,7 @@
     over(REACH, REACH + n - 1, 12, finish)
 
 
-def cycle(meta, table, panel, flags, diagonal, mine, theirs, cases, own, n, total, R):
+def cycle(table, block, mine, theirs, cases, own, n, total, R):
     hops = len(mine)
     extent = n + 2 * REACH
     lanes = table.shape[2]
@@ -287,14 +292,15 @@
         functools.partial(cycle_kernel, tiles=cases // SUB, own_tiles=own // SUB, n=n, total=total, R=R, hops=hops),
         out_shape=(
             jax.ShapeDtypeStruct((own, n * R, lanes), f32),
-            jax.ShapeDtypeStruct((n * R, cases, lanes), f32),
+            jax.ShapeDtypeStruct((n * R // 2, cases, lanes), f32),
+            jax.ShapeDtypeStruct((n * R // 2, cases, lanes), f32),
             jax.ShapeDtypeStruct((n * R, 2 * own, lanes), f32),
         ),
-        in_specs=[pl.BlockSpec(memory_space=pltpu.SMEM)] + [vmem] * (4 + 2 * hops),
-        out_specs=[vmem] * 3,
+        in_specs=[vmem] * (2 + 2 * hops),
+        out_specs=[vmem] * 4,
         scratch_shapes=scratch,
         compiler_params=pltpu.CompilerParams(vmem_limit_bytes=48 * 2**20),
-    )(meta, table, panel, flags, diagonal, *mine, *theirs)
+    )(table, block, *mine, *theirs)
 
 
 def halves(x):
@@ -319,13 +325,19 @@
     return total
 
 
-def near_kernel(left, here, out):
-    out[...] = partial_products(left, here)
-
-
-def far_kernel(meta, left, there, near, out, *, own):
-    here, other = near[...], partial_products(left, there)
-    even_group = meta[1] == 0
+def near_kernel(left, first, second, out):
+    split = first.shape[0]
+    out[...] = partial_products(left, first) + partial_products(left.at[pl.ds(split, split)], second)
+
+
+def early_kernel(left, first, out):
+    out[...] = partial_products(left, first)
+
+
+def late_kernel(left, second, near, early, odd_group, out, *, own):
+    split = second.shape[0]
+    here, other = near[...], early[...] + partial_products(left.at[pl.ds(split, split)], second)
+    even_group = odd_group[...] == 0
     even, odd = jnp.where(even_group, here, other), jnp.where(even_group, other, here)
     parts = []
     for q in range(here.shape[1] // own):
@@ -333,29 +345,31 @@
     out[...] = jnp.concatenate(parts, axis=1)
 
 
-def near_products(left, here):
-    rows, m, lanes = left.shape
-    cases = here.shape[1]
+def product_call(kernel, shape, macs, *operands):
     vmem = pl.BlockSpec(memory_space=pltpu.VMEM)
     return pl.pallas_call(
-        near_kernel,
-        out_shape=jax.ShapeDtypeStruct((m, cases), f32),
-        in_specs=[vmem] * 2,
+        kernel,
+        out_shape=jax.ShapeDtypeStruct(shape, f32),
+        in_specs=[vmem] * len(operands),
         out_specs=vmem,
-        cost_estimate=pl.CostEstimate(flops=6 * rows * m * cases * lanes, bytes_accessed=4 * rows * (m + cases) * lanes, transcendentals=0),
+        cost_estimate=pl.CostEstimate(flops=6 * macs, bytes_accessed=4 * sum(x.size for x in operands), transcendentals=0),
         compiler_params=pltpu.CompilerParams(vmem_limit_bytes=32 * 2**20),
-    )(left, here)
-
-
-def far_products(meta, left, there, near, own):
+    )(*operands)
+
+
+def pack_kernel(panel, flags, diagonal, out):
+    for which, x in enumerate((panel, flags, diagonal)):
+        out[which] = x[...].astype(f32)
+
+
+def pack(panel, flags, diagonal):
     vmem = pl.BlockSpec(memory_space=pltpu.VMEM)
     return pl.pallas_call(
-        functools.partial(far_kernel, own=own),
-        out_shape=jax.ShapeDtypeStruct((near.shape[0], 2 * near.shape[1]), f32),
-        in_specs=[pl.BlockSpec(memory_space=pltpu.SMEM)] + [vmem] * 3,
+        pack_kernel,
+        out_shape=jax.ShapeDtypeStruct((3, *panel.shape), f32),
+        in_specs=[vmem] * 3,
         out_specs=vmem,
-        compiler_params=pltpu.CompilerParams(vmem_limit_bytes=32 * 2**20),
-    )(meta, left, there, near)
+    )(panel, flags, diagonal)
 
 
 def sum_over_slabs(x):
@@ -376,12 +390,11 @@
     slots = groups // 2
     cases = own * slots
     total = n * slabs
-    slab, group = lax.axis_index("slab"), lax.axis_index("case")
-    meta = jnp.stack([slab, group % 2, group // 2]).astype(jnp.int32)
+    group = lax.axis_index("case")
 
     per = SUB // R
     packed = [x.reshape(n // per, SUB, lanes) for x in (panel, flags, diagonal)]
-    block = jnp.stack([x.astype(f32) for x in packed])
+    block = pack(*packed)
     hops = -(-REACH // n)
     mine = []
     for k in range(1, hops + 1):
@@ -398,10 +411,17 @@
     table = lax.dynamic_index_in_dim(table, group % 2, 1, keepdims=False)
     table = table.swapaxes(2, 3).reshape(-1, SUB, lanes)
 
-    fields, worked, left = cycle(meta, table, *packed, mine, theirs, cases, own, n, total, R)
-    received = lax.ppermute(worked, "case", swap)
-    near = near_products(left, worked)
-    sums = sum_over_slabs(far_products(meta, left, received, near, own))
+    fields, first, second, left = cycle(table, block, mine, theirs, cases, own, n, total, R)
+    first_there = lax.ppermute(first, "case", swap)
+    second_there = lax.ppermute(second, "case", swap)
+    part = (2 * own, cases)
+    macs = 2 * own * first.size
+    near = product_call(near_kernel, part, 2 * macs, left, first, second)
+    early = product_call(early_kernel, part, macs, left, first_there)
+    late = functools.partial(late_kernel, own=own)
+    odd_group = jnp.broadcast_to(group % 2, part).astype(jnp.int32)
+    products = product_call(late, (2 * own, 2 * cases), macs, left, second_there, near, early, odd_group)
+    sums = sum_over_slabs(products)
     sums = sums * (1.0 / (total * R * lanes))
     return fields.reshape(own, n, R, lanes), sums[:own], sums[own:]
 

time: 44.5 us -> 43.2 us (0.971)
  other arithmetic: 0.89 us -> 0.01 us
  local copies, waits for them, and re-layouts: 1.35 us -> 0.63 us
    pallas_call x2 -> x4, Pallas kernels: 1.53 us -> 2.55 us  [the longest x1 1.44 us: pack(): pl.pallas_call(pack_kernel, out_shape=jax.ShapeDtypeStruct((3, *panel.sha...]
    convert_element_type x2 -> x0, other arithmetic: 0.79 us -> none  [local(): block = jnp.stack([x.astype(f32) for x in packed])]
    unnamed x8 -> x4, local copies, waits for them, and re-layouts: 0.73 us -> 0.01 us
    ppermute x1 -> x2, waiting for transfers between devices: 1.69 us -> 1.05 us  [the longest x1 0.77 us: local(): first_there = lax.ppermute(first, 'case', swap)]
    pallas_call x1, Pallas kernels: 14.1 us -> 13.5 us  [cycle(): pl.pallas_call(functools.partial(cycle_kernel, tiles=cases // SUB, own_ti...]
  transfers between devices with their start and end apart: 10 -> 11, of which waited for: 6 -> 7; matrix products, arithmetic and copies ran while one was open for 0% -> 0% of each run, Pallas kernels for 1% -> 2%
where the time goes in v4:
time: 43.2 us; the launch traced here: 43.1 us
  Pallas kernels  16.1 us (37%)
  starting transfers between devices  15.5 us (36%)
  waiting for transfers between devices  10.2 us (24%)
  between operations  0.69 us (2%)
  local copies, waits for them, and re-layouts  0.63 us (1%)
    pallas_call x1, Pallas kernels, cycle(): pl.pallas_call(functools.partial(cycle_kernel, tiles=cases // SUB, own_ti...  13.5 us
    ppermute x3, starting transfers between devices, sum_over_slabs(): x = x + lax.ppermute(x, 'slab', [(i, i ^ by) for i in range(count)])  7.41 us
    ppermute x3, starting transfers between devices, local(): mine.append(lax.ppermute(block, ('slab', 'case'), pairs))  7.08 us
    ppermute x3, waiting for transfers between devices, sum_over_slabs(): x = x + lax.ppermute(x, 'slab', [(i, i ^ by) for i in range(count)])  6.09 us
    ppermute x3, waiting for transfers between devices, local(): mine.append(lax.ppermute(block, ('slab', 'case'), pairs))  1.78 us
    pallas_call x1, Pallas kernels, pack(): pl.pallas_call(pack_kernel, out_shape=jax.ShapeDtypeStruct((3, *panel.sha...  1.44 us
    ppermute x3, waiting for transfers between devices, local(): theirs = [lax.ppermute(x, 'case', swap) for x in mine]  1.24 us
    pallas_call x3, Pallas kernels, product_call(): pl.pallas_call(kernel, out_shape=jax.ShapeDtypeStruct(shape, f32), in_spe...  1.1 us
  transfers between devices with their start and end apart: 11, of which 7 were waited for; matrix products, arithmetic and copies ran while one was open for 0% of the time, Pallas kernels for 2%

profile of v4, /device:TPU:0, one launch (start us, length us, event | category | flops | bytes accessed | tf_op | source)
XLA Modules:
  0.0 43.1 jit_solution(12758488390259857948)
XLA Ops:
  0.6 0.0 copy-start
  0.6 1.4 %shard_map.67.block = f32[3,6,8,128]{3,2,1,0:T(8,128)} custom-call(s32[6,8,128]{2,1,0:T(8,128)} %bitcast.12, s32[6,8,128]{2,1,0:T(8,128)} %bitcast.13, f32[6,8,128]{2,1,0:T(8,128)} %bitcast.14), custom_call_target="tpu_custom_call" | custom-call | tf_op jit(solution)/shard_map/pallas_call | solution.py:367
  2.1 3.0 %collective-permute-start = (f32[3,6,8,128]{3,2,1,0:T(8,128)}, f32[3,6,8,128]{3,2,1,0:T(8,128)S(1)}, u32[]{:S(2)}, u32[]{:S(2)}) collective-permute-start(f32[3,6,8,128]{3,2,1,0:T(8,128)} %shard_map.67.block), channel_id=1, source_target_pairs={{0,4},{1,0},{2,6},{3,2},{4,8},{5,1},{6,10},{7,3},{8,12},{9,5},{10,... | collective-permute-start | bytes 221192 | tf_op jit(solution)/shard_map/ppermute | solution.py:406
  5.1 1.6 %collective-permute-start.1 = (f32[3,6,8,128]{3,2,1,0:T(8,128)}, f32[3,6,8,128]{3,2,1,0:T(8,128)S(1)}, u32[]{:S(2)}, u32[]{:S(2)}) collective-permute-start(f32[3,6,8,128]{3,2,1,0:T(8,128)} %shard_map.67.block), channel_id=1, source_target_pairs={{0,8},{1,0},{2,10},{3,2},{4,12},{5,4},{6,14},{7,6},{8,16},{9,1},{1... | collective-permute-start | bytes 221192 | tf_op jit(solution)/shard_map/ppermute | solution.py:406
  6.6 2.5 %collective-permute-start.2 = (f32[3,6,8,128]{3,2,1,0:T(8,128)}, f32[3,6,8,128]{3,2,1,0:T(8,128)S(1)}, u32[]{:S(2)}, u32[]{:S(2)}) collective-permute-start(f32[3,6,8,128]{3,2,1,0:T(8,128)} %shard_map.67.block), channel_id=1, source_target_pairs={{0,12},{1,0},{2,14},{3,2},{4,16},{5,4},{6,18},{7,6},{8,20},{9,8},{... | collective-permute-start | bytes 221192 | tf_op jit(solution)/shard_map/ppermute | solution.py:406
  9.2 0.0 copy-start.1
  9.2 0.0 collective-permute-done.refs_0_
  9.2 0.0 collective-permute-start.3
  9.2 0.0 collective-permute-done.1.refs_1_
  9.2 0.5 %collective-permute-start.4 = (f32[3,6,8,128]{3,2,1,0:T(8,128)S(1)}, f32[3,6,8,128]{3,2,1,0:T(8,128)S(1)}, u32[]{:S(2)}, u32[]{:S(2)}) collective-permute-start(f32[3,6,8,128]{3,2,1,0:T(8,128)S(1)} %collective-permute-done.1.refs_1_), channel_id=1, source_target_pairs={{0,1},{1,0},{2,3},{3,2},{4,5},{5,4},{6,7},{7,6},{8,9},{9,8},{10,11... | collective-permute-start | bytes 221192 | tf_op jit(solution)/shard_map/ppermute | solution.py:408
  9.7 1.8 %collective-permute-done.2.refs_2_ = f32[3,6,8,128]{3,2,1,0:T(8,128)S(1)} collective-permute-done((f32[3,6,8,128]{3,2,1,0:T(8,128)}, f32[3,6,8,128]{3,2,1,0:T(8,128)S(1)}, u32[]{:S(2)}, u32[]{:S(2)}) %collective-permute-start.2) | collective-permute-done | bytes 73760 | tf_op jit(solution)/shard_map/ppermute | solution.py:406
  11.5 0.0 collective-permute-start.5
  11.5 0.0 copy-done
  11.5 0.0 collective-permute-done.3.refs_3_
  11.5 0.0 collective-permute-done.4.refs_4_
  11.5 1.2 %collective-permute-done.5.refs_5_ = f32[3,6,8,128]{3,2,1,0:T(8,128)S(1)} collective-permute-done((f32[3,6,8,128]{3,2,1,0:T(8,128)S(1)}, f32[3,6,8,128]{3,2,1,0:T(8,128)S(1)}, u32[]{:S(2)}, u32[]{:S(2)}) %collective-permute-start.5) | collective-permute-done | bytes 73760 | tf_op jit(solution)/shard_map/ppermute | solution.py:408
  12.7 0.0 copy-done.1
  12.7 13.5 %shard_map.68 = (f32[16,48,128]{2,1,0:T(8,128)}, f32[24,32,128]{2,1,0:T(8,128)S(1)}, f32[24,32,128]{2,1,0:T(8,128)S(1)}, f32[48,32,128]{2,1,0:T(8,128)S(1)}) custom-call(f32[16,8,128]{2,1,0:T(8,128)S(1)} %bitcast.11, f32[3,6,8,128]{3,2,1,0:T(8,128)S(1)} %copy-done.1, f32[3,6,8,128]{3,2,1,0:T(8,128)S(1)} %collective-permute-done.refs_0_, ...), custom_call_target="tpu_custom_call" | custom-call | tf_op jit(solution)/shard_map/pallas_call | solution.py:291
  26.3 0.2 collective-permute-start.7
  26.4 0.4 collective-permute-start.6
  26.8 0.4 %shard_map.69.near = f32[32,32]{1,0:T(8,128)S(1)} custom-call(f32[48,32,128]{2,1,0:T(8,128)S(1)} %get-tuple-element.8.left, f32[24,32,128]{2,1,0:T(8,128)S(1)} %get-tuple-element.10.first, f32[24,32,128]{2,1,0:T(8,128)S(1)} %get-tuple-element.9.second), custom_call_target="tpu_custom_call" | custom-call | flops 37748736 | bytes 1572864 | tf_op jit(solution)/shard_map/pallas_call | solution.py:350
  27.2 0.8 %collective-permute-done.7.first = f32[24,32,128]{2,1,0:T(8,128)S(1)} collective-permute-done((f32[24,32,128]{2,1,0:T(8,128)S(1)}, f32[24,32,128]{2,1,0:T(8,128)S(1)}, u32[]{:S(2)}, u32[]{:S(2)}) %collective-permute-start.7) | collective-permute-done | bytes 393248 | tf_op jit(solution)/shard_map/ppermute | solution.py:415
  28.0 0.3 shard_map.70.early
  28.3 0.3 collective-permute-done.6.second
  28.5 0.4 shard_map.71
  28.9 1.6 %collective-permute-start.8 = (f32[32,64]{1,0:T(8,128)S(1)}, f32[32,64]{1,0:T(8,128)S(1)}, u32[]{:S(2)}, u32[]{:S(2)}) collective-permute-start(f32[32,64]{1,0:T(8,128)S(1)} %shard_map.71), channel_id=1, source_target_pairs={{0,4},{4,0},{8,12},{12,8},{16,20},{20,16},{24,28},{28,24},{1,5},{5... | collective-permute-start | bytes 24584 | tf_op jit(solution)/shard_map/ppermute | solution.py:381
  30.5 2.2 %collective-permute-done.8 = f32[32,64]{1,0:T(8,128)S(1)} collective-permute-done((f32[32,64]{1,0:T(8,128)S(1)}, f32[32,64]{1,0:T(8,128)S(1)}, u32[]{:S(2)}, u32[]{:S(2)}) %collective-permute-start.8) | collective-permute-done | bytes 8224 | tf_op jit(solution)/shard_map/ppermute | solution.py:381
  32.7 1.7 %collective-permute-start.9 = (f32[32,64]{1,0:T(8,128)S(1)}, f32[32,64]{1,0:T(8,128)S(1)}, u32[]{:S(2)}, u32[]{:S(2)}) collective-permute-start(f32[32,64]{1,0:T(8,128)S(1)} %add.20), channel_id=1, source_target_pairs={{0,8},{4,12},{8,0},{12,4},{16,24},{20,28},{24,16},{28,20},{1,9},{5... | collective-permute-start | bytes 24584 | tf_op jit(solution)/shard_map/ppermute | solution.py:381
  34.5 2.0 %collective-permute-done.9 = f32[32,64]{1,0:T(8,128)S(1)} collective-permute-done((f32[32,64]{1,0:T(8,128)S(1)}, f32[32,64]{1,0:T(8,128)S(1)}, u32[]{:S(2)}, u32[]{:S(2)}) %collective-permute-start.9) | collective-permute-done | bytes 8224 | tf_op jit(solution)/shard_map/ppermute | solution.py:381
  36.5 4.1 %collective-permute-start.10 = (f32[32,64]{1,0:T(8,128)S(1)}, f32[32,64]{1,0:T(8,128)S(1)}, u32[]{:S(2)}, u32[]{:S(2)}) collective-permute-start(f32[32,64]{1,0:T(8,128)S(1)} %add.21), channel_id=1, source_target_pairs={{0,16},{4,20},{8,24},{12,28},{16,0},{20,4},{24,8},{28,12},{1,17},{... | collective-permute-start | bytes 24584 | tf_op jit(solution)/shard_map/ppermute | solution.py:381
  40.6 1.8 %collective-permute-done.10 = f32[32,64]{1,0:T(8,128)S(1)} collective-permute-done((f32[32,64]{1,0:T(8,128)S(1)}, f32[32,64]{1,0:T(8,128)S(1)}, u32[]{:S(2)}, u32[]{:S(2)}) %collective-permute-start.10) | collective-permute-done | bytes 8224 | tf_op jit(solution)/shard_map/ppermute | solution.py:381
  42.5 0.6 %fusion = (f32[16,64]{1,0:T(8,128)}, f32[16,64]{1,0:T(8,128)}) fusion(f32[32,64]{1,0:T(8,128)S(1)} %add_multiply_fusion), kind=kLoop, calls=%fused_computation.2 | loop fusion | bytes 16384 | tf_op jit(solution)/shard_map/slice | solution.py:426
  (5 shorter events, 0.0 us)
Async XLA Ops:
  0.6 10.8 %copy-start = (f32[64,512]{1,0:T(8,128)S(1)}, f32[64,512]{1,0:T(8,128)}, u32[]{:S(2)}) copy-start(f32[64,512]{1,0:T(8,128)} %param.4) | copy-start | bytes 393220
  2.1 7.1 %collective-permute-start = (f32[3,6,8,128]{3,2,1,0:T(8,128)}, f32[3,6,8,128]{3,2,1,0:T(8,128)S(1)}, u32[]{:S(2)}, u32[]{:S(2)}) collective-permute-start(f32[3,6,8,128]{3,2,1,0:T(8,128)} %shard_map.67.block), channel_id=1, source_target_pairs={{0,4},{1,0},{2,6},{3,2},{4,8},{5,1},{6,10},{7,3},{8,12},{9,5},{10,... | collective-permute-start | bytes 221192 | tf_op jit(solution)/shard_map/ppermute | solution.py:406
  5.1 4.1 %collective-permute-start.1 = (f32[3,6,8,128]{3,2,1,0:T(8,128)}, f32[3,6,8,128]{3,2,1,0:T(8,128)S(1)}, u32[]{:S(2)}, u32[]{:S(2)}) collective-permute-start(f32[3,6,8,128]{3,2,1,0:T(8,128)} %shard_map.67.block), channel_id=1, source_target_pairs={{0,8},{1,0},{2,10},{3,2},{4,12},{5,4},{6,14},{7,6},{8,16},{9,1},{1... | collective-permute-start | bytes 221192 | tf_op jit(solution)/shard_map/ppermute | solution.py:406
  6.6 4.8 %collective-permute-start.2 = (f32[3,6,8,128]{3,2,1,0:T(8,128)}, f32[3,6,8,128]{3,2,1,0:T(8,128)S(1)}, u32[]{:S(2)}, u32[]{:S(2)}) collective-permute-start(f32[3,6,8,128]{3,2,1,0:T(8,128)} %shard_map.67.block), channel_id=1, source_target_pairs={{0,12},{1,0},{2,14},{3,2},{4,16},{5,4},{6,18},{7,6},{8,20},{9,8},{... | collective-permute-start | bytes 221192 | tf_op jit(solution)/shard_map/ppermute | solution.py:406
  9.2 3.6 %copy-start.1 = (f32[3,6,8,128]{3,2,1,0:T(8,128)S(1)}, f32[3,6,8,128]{3,2,1,0:T(8,128)}, u32[]{:S(2)}) copy-start(f32[3,6,8,128]{3,2,1,0:T(8,128)} %shard_map.67.block) | copy-start | bytes 221188
  9.2 2.3 %collective-permute-start.3 = (f32[3,6,8,128]{3,2,1,0:T(8,128)S(1)}, f32[3,6,8,128]{3,2,1,0:T(8,128)S(1)}, u32[]{:S(2)}, u32[]{:S(2)}) collective-permute-start(f32[3,6,8,128]{3,2,1,0:T(8,128)S(1)} %collective-permute-done.refs_0_), channel_id=1, source_target_pairs={{0,1},{1,0},{2,3},{3,2},{4,5},{5,4},{6,7},{7,6},{8,9},{9,8},{10,11... | collective-permute-start | bytes 221192 | tf_op jit(solution)/shard_map/ppermute | solution.py:408
  9.2 2.3 %collective-permute-start.4 = (f32[3,6,8,128]{3,2,1,0:T(8,128)S(1)}, f32[3,6,8,128]{3,2,1,0:T(8,128)S(1)}, u32[]{:S(2)}, u32[]{:S(2)}) collective-permute-start(f32[3,6,8,128]{3,2,1,0:T(8,128)S(1)} %collective-permute-done.1.refs_1_), channel_id=1, source_target_pairs={{0,1},{1,0},{2,3},{3,2},{4,5},{5,4},{6,7},{7,6},{8,9},{9,8},{10,11... | collective-permute-start | bytes 221192 | tf_op jit(solution)/shard_map/ppermute | solution.py:408
  11.5 1.3 %collective-permute-start.5 = (f32[3,6,8,128]{3,2,1,0:T(8,128)S(1)}, f32[3,6,8,128]{3,2,1,0:T(8,128)S(1)}, u32[]{:S(2)}, u32[]{:S(2)}) collective-permute-start(f32[3,6,8,128]{3,2,1,0:T(8,128)S(1)} %collective-permute-done.2.refs_2_), channel_id=1, source_target_pairs={{0,1},{1,0},{2,3},{3,2},{4,5},{5,4},{6,7},{7,6},{8,9},{9,8},{10,11... | collective-permute-start | bytes 221192 | tf_op jit(solution)/shard_map/ppermute | solution.py:408
  26.3 1.7 %collective-permute-start.7 = (f32[24,32,128]{2,1,0:T(8,128)S(1)}, f32[24,32,128]{2,1,0:T(8,128)S(1)}, u32[]{:S(2)}, u32[]{:S(2)}) collective-permute-start(f32[24,32,128]{2,1,0:T(8,128)S(1)} %get-tuple-element.10.first), channel_id=1, source_target_pairs={{0,1},{1,0},{2,3},{3,2},{4,5},{5,4},{6,7},{7,6},{8,9},{9,8},{10,11... | collective-permute-start | bytes 1179656 | tf_op jit(solution)/shard_map/ppermute | solution.py:415
  26.4 2.1 %collective-permute-start.6 = (f32[24,32,128]{2,1,0:T(8,128)S(1)}, f32[24,32,128]{2,1,0:T(8,128)S(1)}, u32[]{:S(2)}, u32[]{:S(2)}) collective-permute-start(f32[24,32,128]{2,1,0:T(8,128)S(1)} %get-tuple-element.9.second), channel_id=1, source_target_pairs={{0,1},{1,0},{2,3},{3,2},{4,5},{5,4},{6,7},{7,6},{8,9},{9,8},{10,11... | collective-permute-start | bytes 1179656 | tf_op jit(solution)/shard_map/ppermute | solution.py:416
  28.9 3.8 %collective-permute-start.8 = (f32[32,64]{1,0:T(8,128)S(1)}, f32[32,64]{1,0:T(8,128)S(1)}, u32[]{:S(2)}, u32[]{:S(2)}) collective-permute-start(f32[32,64]{1,0:T(8,128)S(1)} %shard_map.71), channel_id=1, source_target_pairs={{0,4},{4,0},{8,12},{12,8},{16,20},{20,16},{24,28},{28,24},{1,5},{5... | collective-permute-start | bytes 24584 | tf_op jit(solution)/shard_map/ppermute | solution.py:381
  32.7 3.7 %collective-permute-start.9 = (f32[32,64]{1,0:T(8,128)S(1)}, f32[32,64]{1,0:T(8,128)S(1)}, u32[]{:S(2)}, u32[]{:S(2)}) collective-permute-start(f32[32,64]{1,0:T(8,128)S(1)} %add.20), channel_id=1, source_target_pairs={{0,8},{4,12},{8,0},{12,4},{16,24},{20,28},{24,16},{28,20},{1,9},{5... | collective-permute-start | bytes 24584 | tf_op jit(solution)/shard_map/ppermute | solution.py:381
  36.5 6.0 %collective-permute-start.10 = (f32[32,64]{1,0:T(8,128)S(1)}, f32[32,64]{1,0:T(8,128)S(1)}, u32[]{:S(2)}, u32[]{:S(2)}) collective-permute-start(f32[32,64]{1,0:T(8,128)S(1)} %add.21), channel_id=1, source_target_pairs={{0,16},{4,20},{8,24},{12,28},{16,0},{20,4},{24,8},{28,12},{1,17},{... | collective-permute-start | bytes 24584 | tf_op jit(solution)/shard_map/ppermute | solution.py:381
